TPU v7x, 32 devices: a whole 2x2x4 slice. The times are simulated.
32 devices in a mesh: mp: 4 (over x, core), dp: 8 (over z, y).
Axes of the slice: x: 2, y: 2, z: 4, core: 2. Of those that a mesh axis runs over, the one named last changes fastest.
Arguments:
- targets: bfloat16 [32, 256, 768], P('dp'), may hold values from -6 to 6
- memory: bfloat16 [32, 1024, 768], P('dp'), may hold values from -6 to 6
- cotangent: bfloat16 [32, 256, 768], P('dp'), may hold values from -6 to 6
- target_len: int32 [32], P('dp'), may hold values from 32 to 256, as said below
- memory_len: int32 [32], P('dp'), may hold values from 128 to 1024, as said below
- query_self: bfloat16 [768, 768], P(None, 'mp'), may hold values from -0.0546875 to 0.0546875
- key_self: bfloat16 [768, 768], P(None, 'mp'), may hold values from -0.21875 to 0.21875
- value_self: bfloat16 [768, 768], P(None, 'mp'), may hold values from -0.21875 to 0.21875
- out_self: bfloat16 [768, 768], P('mp'), may hold values from -1.75 to 1.75
- query_cross: bfloat16 [768, 768], P(None, 'mp'), may hold values from -0.0546875 to 0.0546875
- key_cross: bfloat16 [768, 768], P(None, 'mp'), may hold values from -0.21875 to 0.21875
- value_cross: bfloat16 [768, 768], P(None, 'mp'), may hold values from -0.21875 to 0.21875
- out_cross: bfloat16 [768, 768], P('mp'), may hold values from -1.75 to 1.75
- gate_proj: bfloat16 [768, 2048], P(None, 'mp'), may hold values from -0.21875 to 0.21875
- up_proj: bfloat16 [768, 2048], P(None, 'mp'), may hold values from -0.21875 to 0.21875
- down_proj: bfloat16 [2048, 768], P('mp'), may hold values from -0.1875 to 0.1875
- gain_self: float32 [768], replicated, may hold values from 0.5 to 1.5
- gain_cross: float32 [768], replicated, may hold values from 0.5 to 1.5
- gain_ffn: float32 [768], replicated, may hold values from 0.5 to 1.5
- pos_bias: float32 [32, 12], P(None, 'mp'), may hold values from -4 to 4
Outputs:
- output: bfloat16 [32, 256, 768], P('dp', 'mp')
- grad_targets: bfloat16 [32, 256, 768], P('dp', 'mp')
- grad_memory: bfloat16 [32, 1024, 768], P('dp', 'mp')
- grad_query_self: float32 [768, 768], P('dp', 'mp')
- grad_key_self: float32 [768, 768], P('dp', 'mp')
- grad_value_self: float32 [768, 768], P('dp', 'mp')
- grad_out_self: float32 [768, 768], P('mp', 'dp')
- grad_query_cross: float32 [768, 768], P('dp', 'mp')
- grad_key_cross: float32 [768, 768], P('dp', 'mp')
- grad_value_cross: float32 [768, 768], P('dp', 'mp')
- grad_out_cross: float32 [768, 768], P('mp', 'dp')
- grad_gate: float32 [768, 2048], P('dp', 'mp')
- grad_up: float32 [768, 2048], P('dp', 'mp')
- grad_down: float32 [2048, 768], P('mp', 'dp')
- grad_gain_self: float32 [768], P('dp')
- grad_gain_cross: float32 [768], P('dp')
- grad_gain_ffn: float32 [768], P('dp')
- grad_pos_bias: float32 [32, 12], P(None, 'mp')
Inputs may be any that keep to these rules, and one draw needn't show every extreme that they name: `target_len`: some sequence has exactly 256 target positions and another exactly 32, in every draw. `memory_len`: some sequence has exactly 1024 memory slots and another exactly 128, in every draw.
All inputs are finite; a program needn't handle non-finite values.
Results may differ from a plain program's by a relative error of at most 0.025.
The roundings to bfloat16 on the way count: a program that leaves them out, or rounds other values in their place, can miss the bound.
Values may be sent and summed in bfloat16 or wider, within the bound.
A program may use at most 192 MiB of HBM per device.

v0:
```python
import jax
import jax.numpy as jnp
import numpy as np
from jax import lax
from jax.experimental import pallas as pl
from jax.experimental.pallas import tpu as pltpu
from jax.sharding import PartitionSpec as P

HEAD_DIM = 64
BUCKETS = 32
MAX_DIST = 128


EPS = 1e-06
NEG = -1000000000.0


def bucket_table(length):
    distance = np.maximum(np.arange(length)[:, None] - np.arange(length)[None, :], 0)
    exact = BUCKETS // 2
    scaled = exact + (
        np.log(np.maximum(distance, 1) / exact) / np.log(MAX_DIST / exact) * (BUCKETS - exact)
    ).astype(np.int32)
    return np.where(distance < exact, distance, np.minimum(scaled, BUCKETS - 1)).astype(np.int32)


F32 = jnp.float32
BF16 = jnp.bfloat16
CHUNK = 256
COPIES = 64


def dot(left, right, left_dim, right_dim):
    return lax.dot_general(
        left, right, (((left_dim,), (right_dim,)), ((), ())), preferred_element_type=F32
    )


def dot_nn(left, right):
    return dot(left, right, 1, 0)


def dot_nt(left, right):
    return dot(left, right, 1, 1)


def dot_tn(left, right):
    return dot(left, right, 0, 0)


def unit_rows(resid):
    inv = lax.rsqrt(jnp.mean(resid * resid, -1, keepdims=True) + EPS)
    return inv, resid * inv


def norm_back(resid, gain, grad):
    inv, unit = unit_rows(resid)
    weighted = grad * gain
    grad_resid = inv * (weighted - unit * jnp.mean(weighted * unit, -1, keepdims=True))
    return grad_resid, jnp.sum(grad * unit, 0, keepdims=True)


def layer_kernel(
    tlen_ref, mlen_ref, x0_ref, wq_ref, wk_ref, wv_ref, wo_ref, gains_ref, dist_ref,
    mem_hbm, cot_hbm, xq_hbm, xk_hbm, xv_hbm, xo_hbm, wg_hbm, wu_hbm, wd_hbm,
    out_ref, gt_ref, gm_ref, gf_ref, gx_ref, gs_ref, small_ref,
    q1, k1, v1, e1, r1, u1, o1, bias,
    part_send, part_recv, dn_recv, acc,
    mem, cot, wg, wu, wd, cross_w,
    x1, x2, n2, q2, kv2, e2, r2, u2, o2,
    n3, units, rows_low, rows_recv, rows_send_x, rows_recv_x,
    c2, turned, c1, f_low, f_recv0, f_recv1, f_recv2,
    x_recv0, x_recv1, x_recv2, x_send3, x_recv3,
    s_low, s_recv0, s_recv1, s_recv2, small, small_recv,
    local_sem, send_sem, recv_sem,
):
    me = lax.axis_index("mp")
    core, chip = lax.rem(me, 2), lax.div(me, 2)
    other_core, other_chip = 1 - core, 1 - chip
    by_core = 2 * chip + other_core
    by_x = 2 * other_chip + core
    across = 2 * other_chip + other_core
    at_dp = lax.axis_index("dp")
    bit_y, bit_z1, bit_z2 = lax.rem(at_dp, 2), lax.rem(lax.div(at_dp, 2), 2), lax.div(at_dp, 4)
    by_y = at_dp + 1 - 2 * bit_y
    by_z1 = at_dp + 2 - 4 * bit_z1
    by_z2 = at_dp + 4 - 8 * bit_z2
    to_core, to_x, to_across = {"mp": by_core}, {"mp": by_x}, {"mp": across}
    to_y, to_z1, to_z2 = {"dp": by_y}, {"dp": by_z1}, {"dp": by_z2}

    seqs, length, width = x0_ref.shape
    part = wq_ref.shape[1]
    heads = part // HEAD_DIM
    slots = mem.shape[0]
    blocks = cross_w.shape[0]
    share = width // 8
    quarter = length // blocks

    sent = {}

    def remote(i, src, dst, device):
        return pltpu.make_async_remote_copy(
            src_ref=src, dst_ref=dst, send_sem=send_sem.at[i], recv_sem=recv_sem.at[i],
            device_id=device, device_id_type=pl.DeviceIdType.MESH,
        )

    def send(i, src, dst, device):
        copy = remote(i, src, dst, device)
        copy.start()
        sent[i] = copy

    def left(*names):
        for name in names:
            sent.pop(name).wait_send()

    def arrived(i, dst, device):
        remote(i, dst, dst, device).wait_recv()

    barrier = pltpu.get_barrier_semaphore()
    partners = (to_core, to_x, to_across, to_y, to_z1, to_z2)
    for device in partners:
        pl.semaphore_signal(barrier, inc=1, device_id=device, device_id_type=pl.DeviceIdType.MESH)

    loads = [
        pltpu.make_async_copy(xo_hbm, cross_w.at[me, 3 * part : 4 * part], local_sem.at[3]),
        pltpu.make_async_copy(mem_hbm.at[me], mem, local_sem.at[4]),
        pltpu.make_async_copy(cot_hbm, cot, local_sem.at[5]),
        pltpu.make_async_copy(wg_hbm, wg, local_sem.at[6]),
        pltpu.make_async_copy(wu_hbm, wu, local_sem.at[7]),
        pltpu.make_async_copy(wd_hbm, wd, local_sem.at[8]),
    ]
    staged = [
        pltpu.make_async_copy(
            source.at[i * CHUNK : (i + 1) * CHUNK], stage.at[i], local_sem.at[10 + 3 * j + i]
        )
        for j, (source, stage) in enumerate(((xk_hbm, k1), (xv_hbm, v1), (xq_hbm, q1)))
        for i in range(width // CHUNK)
    ]
    for load in staged + loads:
        load.start()

    key_at = lax.broadcasted_iota(jnp.int32, (length, length), 0)
    query_at = lax.broadcasted_iota(jnp.int32, (length, length), 1)
    for h in range(heads):
        spread = jnp.broadcast_to(dist_ref[h : h + 1, :], (length, length))
        shifted = pltpu.roll(spread, 0, 1, stride=1, stride_axis=0)
        bias[h] = jnp.where(key_at <= query_at, shifted, NEG)

    for load in staged:
        load.wait()
    for j, stage in enumerate((k1, v1, q1)):
        for i in range(width // CHUNK):
            cols = slice(i * CHUNK, (i + 1) * CHUNK)
            cross_w[me, j * part : (j + 1) * part, cols] = stage[i].T
    loads[0].wait()
    pl.semaphore_wait(barrier, len(partners))

    lows, highs = slice(0, 2 * part), slice(2 * part, 4 * part)
    send(0, cross_w.at[me, lows], cross_w.at[me, lows], to_x)
    send(1, cross_w.at[me, lows], cross_w.at[me, lows], to_core)
    send(2, cross_w.at[me, highs], cross_w.at[me, highs], to_x)
    send(3, cross_w.at[me, highs], cross_w.at[me, highs], to_core)

    def self_one(t, carry):
        flip_x, flip_core = 1 - lax.div(t, 2), 1 - lax.rem(t, 2)
        at_x = chip + flip_x - 2 * chip * flip_x
        at_core = core + flip_core - 2 * core * flip_core
        s = 2 * at_x + at_core
        resid = x0_ref[s].astype(F32)
        _, unit = unit_rows(resid)
        n = (unit * gains_ref[0:1, :]).astype(BF16)
        q = dot_nn(n, wq_ref[...]).astype(BF16)
        k = dot_nn(n, wk_ref[...]).astype(BF16)
        v = dot_nn(n, wv_ref[...]).astype(BF16)
        q1[s], k1[s], v1[s] = q, k, v
        mixed = []
        for h in range(heads):
            cols = slice(h * HEAD_DIM, (h + 1) * HEAD_DIM)
            scores = dot_nt(k[:, cols], q[:, cols]) + bias[h]
            scores = jnp.where(key_at < tlen_ref[s], scores, NEG)
            e = jnp.exp(scores - jnp.max(scores, 0, keepdims=True))
            r = 1.0 / jnp.sum(e, 0, keepdims=True)
            e = e.astype(BF16)
            e1[s, h] = e
            r1[s, h] = r
            u = dot_tn(v[:, cols], e)
            u1[s, h] = u
            mixed.append(u * r)
        o = jnp.concatenate(mixed, 0).T.astype(BF16)
        o1[s] = o
        value = dot_nn(o, wo_ref[...])

        @pl.when(t == 0)
        def _():
            part_send[0] = value.astype(BF16)
            remote(4, part_send.at[0], part_recv.at[0], to_core).start()

        @pl.when(t == 1)
        def _():
            arrived(4, part_recv.at[0], to_core)
            part_send[1] = (value + part_recv[0].astype(F32)).astype(BF16)
            remote(5, part_send.at[1], part_recv.at[1], to_x).start()

        @pl.when(t == 2)
        def _():
            part_send[2] = value.astype(BF16)
            remote(6, part_send.at[2], part_recv.at[2], to_core).start()

        @pl.when(t == 3)
        def _():
            x1[...] = resid + value

        return carry

    lax.fori_loop(0, seqs, self_one, 0)
    sent[4] = remote(4, part_send.at[0], part_recv.at[0], to_core)
    sent[5] = remote(5, part_send.at[1], part_recv.at[1], to_x)
    sent[6] = remote(6, part_send.at[2], part_recv.at[2], to_core)

    arrived(0, cross_w.at[by_x, lows], to_x)
    send(7, cross_w.at[by_x, lows], cross_w.at[by_x, lows], to_core)
    arrived(1, cross_w.at[by_core, lows], to_core)
    arrived(7, cross_w.at[across, lows], to_core)
    loads[1].wait()

    def keys_values(b, carry):
        for at in range(0, slots, CHUNK):
            rows = slice(at, at + CHUNK)
            kv2[b, rows, :] = dot_nt(mem[rows, :], cross_w[b, lows, :]).astype(BF16)
        return carry

    lax.fori_loop(0, blocks, keys_values, 0)
    arrived(2, cross_w.at[by_x, highs], to_x)
    send(8, cross_w.at[by_x, highs], cross_w.at[by_x, highs], to_core)
    arrived(3, cross_w.at[by_core, highs], to_core)
    arrived(6, part_recv.at[2], to_core)
    arrived(5, part_recv.at[1], to_x)

    def enter_cross(i, carry):
        rows = pl.ds(pl.multiple_of(i * quarter, quarter), quarter)
        resid = x1[rows, :] + part_recv[1, rows, :].astype(F32) + part_recv[2, rows, :].astype(F32)
        x1[rows, :] = resid
        x2[rows, :] = resid
        n2[rows, :] = (unit_rows(resid)[1] * gains_ref[1:2, :]).astype(BF16)
        return carry

    lax.fori_loop(0, blocks, enter_cross, 0)
    arrived(8, cross_w.at[across, highs], to_core)
    slot_at = lax.broadcasted_iota(jnp.int32, (CHUNK, length), 0)

    def cross_one(b, carry):
        q = dot_nt(n2[...], cross_w[b, 2 * part : 3 * part, :]).astype(BF16)
        q2[b] = q
        mixed = []
        for h in range(heads):
            cols = slice(h * HEAD_DIM, (h + 1) * HEAD_DIM)
            cols_v = slice(part + h * HEAD_DIM, part + (h + 1) * HEAD_DIM)

            def scores_at(at):
                scores = dot_nt(kv2[b, at : at + CHUNK, cols], q[:, cols])
                return jnp.where(slot_at < mlen_ref[me] - at, scores, NEG)

            top = jnp.full((1, length), NEG, F32)
            for at in range(0, slots, CHUNK):
                top = jnp.maximum(top, jnp.max(scores_at(at), 0, keepdims=True))
            total = jnp.zeros((1, length), F32)
            u = jnp.zeros((HEAD_DIM, length), F32)
            for at in range(0, slots, CHUNK):
                rows = slice(at, at + CHUNK)
                e = jnp.exp(scores_at(at) - top)
                total = total + jnp.sum(e, 0, keepdims=True)
                e = e.astype(BF16)
                e2[b * heads + h, rows, :] = e
                u = u + dot_tn(kv2[b, rows, cols_v], e)
            r = 1.0 / total
            r2[b * heads + h] = r
            u2[b * heads + h] = u
            mixed.append(u * r)
        o = jnp.concatenate(mixed, 0).T.astype(BF16)
        o2[b] = o
        x2[...] += dot_nn(o, cross_w[b, 3 * part : 4 * part, :])
        return carry

    lax.fori_loop(0, blocks, cross_one, 0)

    def enter_ffn(i, carry):
        rows = pl.ds(pl.multiple_of(i * quarter, quarter), quarter)
        n3[me, rows, :] = (unit_rows(x2[rows, :])[1] * gains_ref[2:3, :]).astype(BF16)
        return carry

    lax.fori_loop(0, blocks, enter_ffn, 0)
    send(9, n3.at[me], n3.at[me], to_x)
    send(10, n3.at[me], n3.at[me], to_core)
    for load in loads[2:]:
        load.wait()
    left(4, 5, 6)
    scale, cubic = 0.7978845608028654, 0.044715

    def ffn_one(t, carry):
        flip_x, flip_core = lax.div(t, 2), lax.rem(t, 2)
        at_x = chip + flip_x - 2 * chip * flip_x
        at_core = core + flip_core - 2 * core * flip_core
        s = 2 * at_x + at_core

        @pl.when(t == 1)
        def _():
            arrived(10, n3.at[by_core], to_core)

        @pl.when(t == 2)
        def _():
            arrived(9, n3.at[by_x], to_x)
            remote(11, n3.at[by_x], n3.at[by_x], to_core).start()

        @pl.when(t == 3)
        def _():
            arrived(11, n3.at[across], to_core)

        n, c = n3[s], cot[s]
        rows = pl.ds(pl.multiple_of(s * length, length), length)
        for at in range(0, wg.shape[1], CHUNK):
            cols = slice(at, at + CHUNK)
            a = dot_nn(n, wg[:, cols])
            b = dot_nn(n, wu[:, cols])
            dh = dot_nt(c, wd[cols, :])
            square = a * a
            slope = jnp.tanh(scale * (a + cubic * (a * square)))
            half = 0.5 * (1.0 + slope)
            gelu = a * half
            rise = half + 0.5 * a * (1.0 - slope * slope) * (scale * (1.0 + 3.0 * cubic * square))
            units[0, rows, cols] = (dh * b * rise).astype(BF16)
            units[1, rows, cols] = (dh * gelu).astype(BF16)
            units[2, rows, cols] = (gelu * b).astype(BF16)
        dn = dot_nt(units[0, rows, :], wg[...]) + dot_nt(units[1, rows, :], wu[...])

        @pl.when(t == 0)
        def _():
            acc[...] = dn

        @pl.when(t == 1)
        def _():
            part_send[0] = dn.astype(BF16)
            remote(12, part_send.at[0], dn_recv.at[0], to_core).start()

        @pl.when(t == 2)
        def _():
            part_send[2] = dn.astype(BF16)

        @pl.when(t == 3)
        def _():
            part_send[1] = dn.astype(BF16)
            remote(13, part_send.at[1], dn_recv.at[1], to_core).start()

        own = jnp.where(t == 0, 1.0, 0.0)
        result = dot_nn(units[2, rows, :], wd[...]) + own * x2[...]
        for i in range(blocks):
            rows_low[i % 2, i // 2, s] = result[i * quarter : (i + 1) * quarter].astype(BF16)
        return carry

    lax.fori_loop(0, seqs, ffn_one, 0)
    sent[11] = remote(11, n3.at[by_x], n3.at[by_x], to_core)
    arrived(13, dn_recv.at[1], to_core)
    part_send[2] = (part_send[2].astype(F32) + dn_recv[1].astype(F32)).astype(BF16)
    send(14, part_send.at[2], dn_recv.at[2], to_x)
    sent[12] = remote(12, part_send.at[0], dn_recv.at[0], to_core)
    sent[13] = remote(13, part_send.at[1], dn_recv.at[1], to_core)
    send(15, rows_low.at[other_core], rows_recv, to_core)

    def turn(slot, value, first_col, order):
        value = value.T
        for j in range(8):
            y, z1, z2 = j % 2, j // 2 % 2, j // 4
            at = (4 * y + 2 * z1 + z2) if order == "y" else (4 * z1 + 2 * y + z2)
            cols = slice(first_col, first_col + value.shape[1])
            turned[slot, at * share : (at + 1) * share, cols] = value[j * share : (j + 1) * share]

    for s in range(seqs):
        turn(0, n3[s], s * length, "y")
        turn(1, cot[s], s * length, "y")

    half_rows = 4 * share

    def half_at(bit):
        return pl.ds(pl.multiple_of(bit * half_rows, half_rows), half_rows)

    for keep in (False, True):
        for i in range(3):
            rows = half_at(bit_y if keep else 1 - bit_y)
            f_low[i, rows, :] = dot_nn(turned[i // 2, rows, :], units[i]).astype(BF16)
            if not keep:
                send(16 + i, f_low.at[i, rows], f_recv0.at[i], to_y)

    arrived(15, rows_recv, to_core)
    rows_send_x[...] = (
        rows_low[core, other_chip].astype(F32) + rows_recv[other_chip].astype(F32)
    ).astype(BF16)
    send(19, rows_send_x, rows_recv_x, to_x)

    arrived(12, dn_recv.at[0], to_core)
    arrived(14, dn_recv.at[2], to_x)
    small[...] = jnp.zeros_like(small)

    def enter_back(i, carry):
        rows = pl.ds(pl.multiple_of(i * quarter, quarter), quarter)
        dn3 = acc[rows, :] + dn_recv[0, rows, :].astype(F32) + dn_recv[2, rows, :].astype(F32)
        grad, gain_ffn = norm_back(x2[rows, :], gains_ref[2:3, :], dn3)
        dx2 = cot[me, rows, :].astype(F32) + grad
        acc[rows, :] = dx2
        c2[rows, :] = dx2.astype(BF16)
        small[0, 2:3, :] += gain_ffn
        return carry

    lax.fori_loop(0, blocks, enter_back, 0)

    def cross_back(b, carry):
        do = dot_nt(cross_w[b, 3 * part : 4 * part, :], c2[...])
        q = q2[b]
        dqs = []
        for h in range(heads):
            cols = slice(h * HEAD_DIM, (h + 1) * HEAD_DIM)
            cols_v = slice(part + h * HEAD_DIM, part + (h + 1) * HEAD_DIM)
            r = r2[b * heads + h]
            low = (do[cols] * r).astype(BF16)
            delta = r * jnp.sum(low.astype(F32) * u2[b * heads + h], 0, keepdims=True)
            dq = jnp.zeros((HEAD_DIM, length), F32)
            for at in range(0, slots, CHUNK):
                rows = slice(at, at + CHUNK)
                e = e2[b * heads + h, rows, :]
                dp = dot_nn(kv2[b, rows, cols_v], low)
                ds = (e.astype(F32) * (dp - delta)).astype(BF16)
                dq = dq + dot_tn(kv2[b, rows, cols], ds)
                kv2[b, rows, cols_v] = dot_nt(e, low).astype(BF16)
                kv2[b, rows, cols] = dot_nn(ds, q[:, cols]).astype(BF16)
            dqs.append(dq)
        q2[b] = jnp.concatenate(dqs, 0).T.astype(BF16)
        return carry

    lax.fori_loop(0, blocks, cross_back, 0)
    dn2 = dot_nn(q2[0], cross_w[0, 2 * part : 3 * part, :])
    for b in range(1, blocks):
        dn2 = dn2 + dot_nn(q2[b], cross_w[b, 2 * part : 3 * part, :])
    x2[...] = dn2

    def leave_cross(i, carry):
        rows = pl.ds(pl.multiple_of(i * quarter, quarter), quarter)
        grad, gain_cross = norm_back(x1[rows, :], gains_ref[1:2, :], x2[rows, :])
        c1[me, rows, :] = (acc[rows, :] + grad).astype(BF16)
        small[0, 1:2, :] += gain_cross
        return carry

    lax.fori_loop(0, blocks, leave_cross, 0)
    arrived(19, rows_recv_x, to_x)
    out_ref[...] = (
        rows_low[core, chip].astype(F32)
        + rows_recv[chip].astype(F32)
        + rows_recv_x[...].astype(F32)
    ).astype(BF16)
    left(15, 19)
    send(20, c1.at[me], c1.at[me], to_x)
    send(21, c1.at[me], c1.at[me], to_core)

    def add_rows(ref, start, count, recv, recv_start):
        at = pl.ds(pl.multiple_of(start, share), count)
        from_at = pl.ds(pl.multiple_of(recv_start, share), count)
        ref[at, :] = (ref[at, :].astype(F32) + recv[from_at, :].astype(F32)).astype(BF16)

    def pass_on(ref, base, count, recv, bit, i, recv_next, device):
        away, kept = (1 - bit) * count, bit * count
        add_rows(ref, base + away, count, recv, away)
        rows = pl.ds(pl.multiple_of(base + away, share), count)
        send(i, ref.at[rows], recv_next, device)
        add_rows(ref, base + kept, count, recv, kept)
        return base + kept

    f_base = [None] * 3
    for i in range(3):
        arrived(16 + i, f_recv0.at[i], to_y)
        f_base[i] = pass_on(
            f_low.at[i], bit_y * half_rows, 2 * share, f_recv0.at[i], bit_z1, 22 + i, f_recv1.at[i], to_z1
        )

    left(9, 10, 11)

    def memory_grad(target):
        rows = pl.ds(pl.multiple_of(target * CHUNK, CHUNK), CHUNK)
        total = None
        for b in range(blocks):
            term = dot_nn(kv2[b, rows, :], cross_w[b, lows, :])
            total = term if total is None else total + term
        n3[target] = total.astype(BF16)

    memory_grad(by_x)
    send(25, n3.at[by_x], gm_ref.at[me], to_x)
    memory_grad(across)
    send(26, n3.at[across], gm_ref.at[me], to_across)
    memory_grad(by_core)
    send(27, n3.at[by_core], gm_ref.at[me], to_core)
    memory_grad(me)
    own_rows = pltpu.make_async_copy(n3.at[me], gm_ref.at[me], local_sem.at[9])
    own_rows.start()

    turn(0, mem[...], 0, "z1")
    turn(1, n2[...], 0, "z1")
    turn(1, c2[...], length, "z1")
    arrived(21, c1.at[by_core], to_core)

    def cross_grads(b):
        for at in range(0, width, half_rows):
            rows = slice(at, at + half_rows)
            kv = dot_nn(turned[0, rows, :], kv2[b]).astype(BF16)
            q = dot_nn(turned[1, rows, 0:length], q2[b]).astype(BF16)
            o = dot_nn(turned[1, rows, length : 2 * length], o2[b]).astype(BF16)
            e2[3 * b, rows, :] = kv[:, 0:256]
            e2[3 * b + 1, rows, 0:128] = kv[:, 256:384]
            e2[3 * b + 1, rows, 128:256] = q[:, 0:128]
            e2[3 * b + 2, rows, 0:64] = q[:, 128:192]
            e2[3 * b + 2, rows, 64:256] = o

    for i in range(2):
        b = 2 * i + other_core
        cross_grads(b)
        for j in range(3):
            send(
                28 + 3 * i + j,
                e2.at[3 * b + j, 0:width],
                units.at[j, 0:width, 256 * i : 256 * (i + 1)],
                to_core,
            )
    arrived(20, c1.at[by_x], to_x)
    send(34, c1.at[by_x], c1.at[by_x], to_core)
    for i in range(2):
        cross_grads(2 * i + core)
    for i in range(2):
        b = 2 * i + core
        for j in range(3):
            arrived(28 + 3 * i + j, units.at[j, 0:width, 256 * i : 256 * (i + 1)], to_core)
            landed = units.at[j, 0:width, 256 * i : 256 * (i + 1)]
            mine = e2.at[3 * b + j, 0:width]
            add_rows(mine, (1 - bit_z1) * half_rows, half_rows, landed, (1 - bit_z1) * half_rows)
        send(
            35 + i,
            e2.at[pl.ds(3 * b, 3), half_at(1 - bit_z1)],
            x_recv0.at[i],
            to_z1,
        )
        for j in range(3):
            landed = units.at[j, 0:width, 256 * i : 256 * (i + 1)]
            mine = e2.at[3 * b + j, 0:width]
            add_rows(mine, bit_z1 * half_rows, half_rows, landed, bit_z1 * half_rows)

    bias[...] = jnp.zeros_like(bias)

    def self_back(t, carry):
        flip_x, flip_core = lax.div(t, 2), lax.rem(t, 2)
        at_x = chip + flip_x - 2 * chip * flip_x
        at_core = core + flip_core - 2 * core * flip_core
        s = 2 * at_x + at_core

        @pl.when(t == 3)
        def _():
            arrived(34, c1.at[across], to_core)

        do = dot_nt(wo_ref[...], c1[s])
        dqs = []
        for h in range(heads):
            cols = slice(h * HEAD_DIM, (h + 1) * HEAD_DIM)
            r = r1[s, h]
            low = (do[cols] * r).astype(BF16)
            delta = r * jnp.sum(low.astype(F32) * u1[s, h], 0, keepdims=True)
            e = e1[s, h]
            dp = dot_nn(v1[s, :, cols], low)
            ds = (e.astype(F32) * (dp - delta)).astype(BF16)
            bias[h] += ds.astype(F32)
            dqs.append(dot_tn(k1[s, :, cols], ds))
            v1[s, :, cols] = dot_nt(e, low).astype(BF16)
            k1[s, :, cols] = dot_nn(ds, q1[s, :, cols]).astype(BF16)
        q1[s] = jnp.concatenate(dqs, 0).T.astype(BF16)
        dn = dot_nt(q1[s], wq_ref[...]) + dot_nt(k1[s], wk_ref[...]) + dot_nt(v1[s], wv_ref[...])
        acc[...] = dn
        for i in range(blocks):
            rows = slice(i * quarter, (i + 1) * quarter)
            unit = unit_rows(x0_ref[s, rows, :].astype(F32))[1]
            small[0, 0:1, :] += jnp.sum(acc[rows, :] * unit, 0, keepdims=True)
            rows_low[i % 2, i // 2, s] = acc[rows, :].astype(BF16)
        return carry

    lax.fori_loop(0, seqs, self_back, 0)
    send(37, rows_low.at[other_core], rows_recv, to_core)
    send(38, small.at[0], small_recv.at[0], to_core)

    for s in range(seqs):
        _, unit = unit_rows(x0_ref[s].astype(F32))
        turn(0, (unit * gains_ref[0:1, :]).astype(BF16), s * length, "y")
        turn(1, c1[s], s * length, "y")
    for keep in (False, True):
        rows = half_at(bit_y if keep else 1 - bit_y)
        for i, ref in enumerate((k1, v1, q1, o1)):
            right = ref[...].reshape(seqs * length, part)
            value = dot_nn(turned[1 if i == 3 else 0, rows, :], right).astype(BF16)
            s_low[rows, i * part : (i + 1) * part] = value
        if not keep:
            send(39, s_low.at[rows], s_recv0, to_y)

    arrived(37, rows_recv, to_core)
    rows_send_x[...] = (
        rows_low[core, other_chip].astype(F32) + rows_recv[other_chip].astype(F32)
    ).astype(BF16)
    send(40, rows_send_x, rows_recv_x, to_x)
    arrived(38, small_recv.at[0], to_core)
    small[1, 0:8] = small[0] + small_recv[0]
    send(41, small.at[1], small_recv.at[1], to_x)
    for h in range(heads):
        total = bias[h]
        step = 1
        while step < length:
            total = jnp.where((key_at & step) != 0, pltpu.roll(total, length - step, 1), total)
            step *= 2
        small[3, h : h + 1, 0:length] = jnp.sum(total, 0, keepdims=True)
    arrived(41, small_recv.at[1], to_x)
    small[2] = small[1] + small_recv[1]
    send(42, small.at[pl.ds(2, 2)], small_recv.at[pl.ds(2, 2)], to_y)

    x_base = [None] * 2
    for i in range(3):
        arrived(22 + i, f_recv1.at[i], to_z1)
        f_base[i] = pass_on(
            f_low.at[i], f_base[i], share, f_recv1.at[i], bit_z2, 47 + i, f_recv2.at[i], to_z2
        )
    for i in range(2):
        b = 2 * i + core
        arrived(35 + i, x_recv0.at[i], to_z1)
        base = bit_z1 * half_rows
        away, kept = base + (1 - bit_y) * 2 * share, base + bit_y * 2 * share
        for j in range(3):
            add_rows(e2.at[3 * b + j], away, 2 * share, x_recv0.at[i, j], (1 - bit_y) * 2 * share)
        send(
            50 + i,
            e2.at[pl.ds(3 * b, 3), pl.ds(pl.multiple_of(away, share), 2 * share)],
            x_recv1.at[i],
            to_y,
        )
        for j in range(3):
            add_rows(e2.at[3 * b + j], kept, 2 * share, x_recv0.at[i, j], bit_y * 2 * share)
        x_base[i] = kept

    arrived(42, small_recv.at[pl.ds(2, 2)], to_y)
    small[4:6] = small[2:4] + small_recv[2:4]
    send(44, small.at[pl.ds(4, 2)], small_recv.at[pl.ds(4, 2)], to_z1)
    arrived(39, s_recv0, to_y)
    s_base = pass_on(s_low, bit_y * half_rows, 2 * share, s_recv0, bit_z1, 52, s_recv1, to_z1)

    for i in range(2):
        b = 2 * i + core
        arrived(50 + i, x_recv1.at[i], to_y)
        away, kept = x_base[i] + (1 - bit_z2) * share, x_base[i] + bit_z2 * share
        for j in range(3):
            add_rows(e2.at[3 * b + j], away, share, x_recv1.at[i, j], (1 - bit_z2) * share)
        send(
            53 + i,
            e2.at[pl.ds(3 * b, 3), pl.ds(pl.multiple_of(away, share), share)],
            x_recv2.at[i],
            to_z2,
        )
        for j in range(3):
            add_rows(e2.at[3 * b + j], kept, share, x_recv1.at[i, j], bit_z2 * share)
        x_base[i] = kept

    base = x_base[0]

    def cross_sum(at):
        rows = pl.ds(pl.multiple_of(base, share), share)
        return [
            e2[3 * (2 * at + core) + j, rows, :].astype(F32) + x_recv2[at, j].astype(F32)
            for j in range(3)
        ]

    arrived(40, rows_recv_x, to_x)
    my_rows = pl.ds(pl.multiple_of(me * quarter, quarter), quarter)
    for s in range(seqs):
        dn = (
            rows_low[core, chip, s].astype(F32)
            + rows_recv[chip, s].astype(F32)
            + rows_recv_x[s].astype(F32)
        )
        grad, _ = norm_back(x0_ref[s, my_rows, :].astype(F32), gains_ref[0:1, :], dn)
        gt_ref[s] = (c1[s, my_rows, :].astype(F32) + grad).astype(BF16)

    arrived(44, small_recv.at[pl.ds(4, 2)], to_z1)
    small[6:8] = small[4:6] + small_recv[4:6]
    send(46, small.at[pl.ds(6, 2)], small_recv.at[pl.ds(6, 2)], to_z2)
    arrived(52, s_recv1, to_z1)
    s_base = pass_on(s_low, s_base, share, s_recv1, bit_z2, 55, s_recv2, to_z2)
    for i in range(2):
        arrived(53 + i, x_recv2.at[i], to_z2)
    for j, value in enumerate(cross_sum(other_chip)):
        x_send3[j] = value.astype(BF16)
    send(56, x_send3, x_recv3, to_x)
    for i in range(3):
        arrived(47 + i, f_recv2.at[i], to_z2)
        rows = pl.ds(pl.multiple_of(f_base[i], share), share)
        gf_ref[i] = f_low[i, rows, :].astype(F32) + f_recv2[i].astype(F32)
    arrived(46, small_recv.at[pl.ds(6, 2)], to_z2)
    small_ref[...] = small[6:8] + small_recv[6:8]
    arrived(55, s_recv2, to_z2)
    rows = pl.ds(pl.multiple_of(s_base, share), share)
    gs_ref[...] = s_low[rows, :].astype(F32) + s_recv2[...].astype(F32)
    arrived(56, x_recv3, to_x)
    for j, value in enumerate(cross_sum(chip)):
        gx_ref[j] = value + x_recv3[j].astype(F32)
    arrived(25, gm_ref.at[by_x], to_x)
    arrived(26, gm_ref.at[across], to_across)
    arrived(27, gm_ref.at[by_core], to_core)
    own_rows.wait()
    for copy in sent.values():
        copy.wait_send()


def finish_kernel(
    gf_ref, gx_ref, gs_ref, small_ref, onehot_ref, out_ref, gt_ref, gm_ref,
    out_o, gt_o, gm_o, sq_o, sk_o, sv_o, so_o, cq_o, ck_o, cv_o, co_o, gg_o, gu_o, gd_o,
    gains_o, bias_o,
):
    part = sq_o.shape[1]
    out_o[...], gt_o[...], gm_o[...] = out_ref[...], gt_ref[...], gm_ref[...]
    gg_o[...], gu_o[...], gd_o[...] = gf_ref[0], gf_ref[1], gf_ref[2].T
    whole = jnp.concatenate([gx_ref[0], gx_ref[1], gx_ref[2]], 1)
    for value, refs in ((whole, (ck_o, cv_o, cq_o, co_o)), (gs_ref[...], (sk_o, sv_o, sq_o, so_o))):
        for i in range(3):
            refs[i][...] = value[:, i * part : (i + 1) * part]
        refs[3][...] = value[:, 3 * part :].T
    gains_o[...] = small_ref[0]
    bias_o[...] = lax.dot_general(
        onehot_ref[...], small_ref[1, :, 0 : onehot_ref.shape[0]], (((0,), (1,)), ((), ())),
        precision=lax.Precision.HIGHEST, preferred_element_type=F32,
    )


VMEM = pl.BlockSpec(memory_space=pltpu.VMEM)
SMEM = pl.BlockSpec(memory_space=pltpu.SMEM)
ANY = pl.BlockSpec(memory_space=pl.ANY)


def on_device(
    targets,
    memory,
    cotangent,
    target_len,
    memory_len,
    query_self,
    key_self,
    value_self,
    out_self,
    query_cross,
    key_cross,
    value_cross,
    out_cross,
    gate_proj,
    up_proj,
    down_proj,
    gain_self,
    gain_cross,
    gain_ffn,
    pos_bias,
):
    seqs, length, width = targets.shape
    slots = memory.shape[1]
    part = query_self.shape[1]
    units = gate_proj.shape[1]
    heads = part // HEAD_DIM
    blocks = lax.axis_size("mp")
    dp_size = lax.axis_size("dp")
    share = width // dp_size
    quarter = length // blocks
    head_all = heads * blocks

    onehot = jnp.asarray(
        (bucket_table(length)[:, 0][:, None] == np.arange(BUCKETS)[None, :]).astype(np.float32)
    )
    dist = jnp.dot(onehot, pos_bias, precision=lax.Precision.HIGHEST).T
    gains = jnp.stack([gain_self, gain_cross, gain_ffn])

    def low(*shape):
        return pltpu.VMEM(shape, BF16)

    def full(*shape):
        return pltpu.VMEM(shape, F32)

    def sums(count, columns):
        return [low(count, 4 * share, columns), low(count, 2 * share, columns), low(count, share, columns)]

    scratch = [
        low(seqs, length, part), low(seqs, length, part), low(seqs, length, part),
        low(seqs, heads, length, length), full(seqs, heads, 1, length),
        full(seqs, heads, HEAD_DIM, length), low(seqs, length, part), full(heads, length, length),
        low(3, length, width), low(3, length, width), low(3, length, width),
        full(length, width),
        low(slots, width), low(seqs, length, width),
        low(width, units), low(width, units), low(units, width), low(blocks, 4 * part, width),
        full(length, width), full(length, width), low(length, width), low(blocks, length, part),
        low(blocks, slots, 2 * part), low(head_all, slots, length), full(head_all, 1, length),
        full(head_all, HEAD_DIM, length), low(blocks, length, part),
        low(seqs, length, width), low(3, seqs * length, units),
        low(2, 2, seqs, quarter, width), low(2, seqs, quarter, width),
        low(seqs, quarter, width), low(seqs, quarter, width),
        low(length, width), low(2, width, seqs * length), low(seqs, length, width),
        low(3, width, units), *sums(3, units),
        low(2, 3, 4 * share, 256), low(2, 3, 2 * share, 256), low(2, 3, share, 256),
        low(3, share, 256), low(3, share, 256),
        low(width, width), low(4 * share, width), low(2 * share, width), low(share, width),
        full(8, 8, width), full(8, 8, width),
        pltpu.SemaphoreType.DMA((19,)),
        pltpu.SemaphoreType.DMA((COPIES,)),
        pltpu.SemaphoreType.DMA((COPIES,)),
    ]
    struct = jax.ShapeDtypeStruct
    rows = struct((seqs, quarter, width), BF16)
    out, gt, gm, gf, gx, gs, small = pl.pallas_call(
        layer_kernel,
        out_shape=[
            rows,
            rows,
            struct((seqs, slots // blocks, width), BF16),
            struct((3, share, units), F32),
            struct((3, share, 256), F32),
            struct((share, width), F32),
            struct((2, 8, width), F32),
        ],
        in_specs=[SMEM] * 2 + [VMEM] * 7 + [ANY] * 9,
        out_specs=[VMEM, VMEM, ANY, VMEM, VMEM, VMEM, VMEM],
        scratch_shapes=scratch,
        compiler_params=pltpu.CompilerParams(
            collective_id=0, has_side_effects=True, vmem_limit_bytes=63 * 2**20
        ),
        cost_estimate=pl.CostEstimate(flops=24 * 10**9, bytes_accessed=2**24, transcendentals=0),
        name="layer",
    )(
        target_len, memory_len, targets, query_self, key_self, value_self, out_self, gains, dist,
        memory, cotangent, query_cross, key_cross, value_cross, out_cross,
        gate_proj, up_proj, down_proj,
    )
    square = struct((share, part), F32)
    turned = struct((part, share), F32)
    (
        out, gt, gm, sq, sk, sv, so, cq, ck, cv, co, gg, gu, gd, gains, bias,
    ) = pl.pallas_call(
        finish_kernel,
        out_shape=[
            rows, rows, struct((seqs, slots // blocks, width), BF16),
            square, square, square, turned, square, square, square, turned,
            struct((share, units), F32), struct((share, units), F32), struct((units, share), F32),
            struct((8, width), F32), struct((BUCKETS, 8), F32),
        ],
        in_specs=[VMEM] * 8,
        out_specs=[VMEM] * 16,
        compiler_params=pltpu.CompilerParams(vmem_limit_bytes=32 * 2**20),
        name="finish",
    )(gf, gx, gs, small, onehot, out, gt, gm)
    gains = lax.dynamic_slice_in_dim(gains[:3], lax.axis_index("dp") * share, share, 1)
    return (
        out, gt, gm, sq, sk, sv, so, cq, ck, cv, co, gg, gu, gd,
        gains[0], gains[1], gains[2], bias[:, :heads],
    )


def project(inputs, weight):
    return jnp.einsum("bld,df->blf", inputs, weight, preferred_element_type=jnp.float32)


def back_project(gradient, weight):
    return jnp.einsum("blf,df->bld", gradient, weight, preferred_element_type=jnp.float32)


def weight_grad(inputs, gradient):
    return jnp.einsum("bld,blf->df", inputs, gradient, preferred_element_type=jnp.float32)


def norm_forward(resid, gain):
    inv_rms = lax.rsqrt(jnp.mean(resid * resid, -1, keepdims=True) + EPS)
    return (resid * inv_rms * gain, inv_rms)


def norm_backward(resid, inv_rms, gain, grad_normed):
    unit_rows = resid * inv_rms
    grad_gain = jnp.sum(grad_normed * unit_rows, axis=(0, 1))
    weighted = grad_normed * gain
    grad_resid = inv_rms * (
        weighted - unit_rows * jnp.mean(weighted * unit_rows, -1, keepdims=True)
    )
    return (grad_resid, grad_gain)


def scores_of(queries, keys, score_bias, valid):
    scores = (
        jnp.einsum("bihe,bjhe->bhij", queries, keys, preferred_element_type=jnp.float32)
        + score_bias
    )
    return jnp.where(valid, scores, NEG)


def attend(queries, keys, values, score_bias, valid):
    scores = scores_of(queries, keys, score_bias, valid)
    row_max = jnp.max(scores, -1, keepdims=True)
    log_total = row_max + jnp.log(jnp.sum(jnp.exp(scores - row_max), -1, keepdims=True))
    attn_probs = jnp.exp(scores - log_total).astype(jnp.bfloat16)
    mixed = jnp.einsum("bhij,bjhe->bihe", attn_probs, values, preferred_element_type=jnp.float32)
    return (mixed, log_total)


def attend_back(queries, keys, values, score_bias, valid, log_total, grad_mixed):
    attn_probs = jnp.exp(scores_of(queries, keys, score_bias, valid) - log_total)
    grad_values = jnp.einsum(
        "bhij,bihe->bjhe",
        attn_probs.astype(jnp.bfloat16),
        grad_mixed,
        preferred_element_type=jnp.float32,
    )
    grad_probs = jnp.einsum(
        "bihe,bjhe->bhij", grad_mixed, values, preferred_element_type=jnp.float32
    )
    grad_scores = attn_probs * (grad_probs - jnp.sum(attn_probs * grad_probs, -1, keepdims=True))
    grad_low = grad_scores.astype(jnp.bfloat16)
    grad_queries = jnp.einsum("bhij,bjhe->bihe", grad_low, keys, preferred_element_type=jnp.float32)
    grad_keys = jnp.einsum("bhij,bihe->bjhe", grad_low, queries, preferred_element_type=jnp.float32)
    return (grad_queries, grad_keys, grad_values, grad_low)


def swap(value, axis, bit):
    return lax.ppermute(value, axis, [(i, i ^ bit) for i in range(lax.axis_size(axis))])


def bits_of(axis):
    return [1 << i for i in range(lax.axis_size(axis).bit_length() - 1)]


def split_bits(value, axis, dim):
    steps = len(bits_of(axis))
    shape = value.shape
    return value.reshape(
        shape[:dim] + (2,) * steps + (shape[dim] >> steps,) + shape[dim + 1 :]
    )


def own_bit(axis, bit):
    return (lax.axis_index(axis) & bit) // bit


def halve(value, axis, bit, dim):
    mine = own_bit(axis, bit)
    kept = lax.dynamic_index_in_dim(value, mine, dim, keepdims=False)
    sent = lax.dynamic_index_in_dim(value, 1 - mine, dim, keepdims=False)
    arrived = swap(sent.astype(jnp.bfloat16), axis, bit)
    return kept + arrived.astype(jnp.float32)


def reduce_scatter(value, axis, dim):
    bits = bits_of(axis)
    value = split_bits(value, axis, dim)
    for at, bit in enumerate(bits):
        value = halve(value, axis, bit, dim + len(bits) - 1 - at)
    return value


def gather_mp(value):
    value = value[None]
    for bit in reversed(bits_of("mp")):
        other = swap(value, "mp", bit)
        first = own_bit("mp", bit) == 0
        low = jnp.where(first, value, other)
        high = jnp.where(first, other, value)
        value = jnp.stack([low, high], 1 if bit == 1 else 0)
        value = value.reshape((-1,) + value.shape[2:])
    return value


def exchange_mp(value):
    count = lax.axis_size("mp")
    value = split_bits(value, "mp", 0)[None]
    steps = len(bits_of("mp"))
    for at, bit in enumerate(bits_of("mp")):
        dim = steps - at
        mine = own_bit("mp", bit)
        kept = lax.dynamic_index_in_dim(value, mine, dim, keepdims=False)
        sent = lax.dynamic_index_in_dim(value, 1 - mine, dim, keepdims=False)
        arrived = swap(sent, "mp", bit)
        first = mine == 0
        low = jnp.where(first, kept, arrived)
        high = jnp.where(first, arrived, kept)
        value = jnp.stack([low, high], 0)
        value = value.reshape((-1,) + value.shape[2:])
    return value.reshape((count,) + value.shape[1:])


def sum_mp(value):
    for bit in bits_of("mp"):
        value = value + swap(value, "mp", bit)
    return value


def on_device_permutes(
    targets,
    memory,
    cotangent,
    target_len,
    memory_len,
    query_self,
    key_self,
    value_self,
    out_self,
    query_cross,
    key_cross,
    value_cross,
    out_cross,
    gate_proj,
    up_proj,
    down_proj,
    gain_self,
    gain_cross,
    gain_ffn,
    pos_bias,
):
    length = targets.shape[1]
    heads_local = query_self.shape[1] // HEAD_DIM
    mp_size = lax.axis_size("mp")
    dp_size = lax.axis_size("dp")
    mp_index = lax.axis_index("mp")
    row_share = length // mp_size
    width = targets.shape[2]

    def split_heads(value):
        return value.reshape(value.shape[0], value.shape[1], -1, HEAD_DIM)

    def merge_heads(value):
        return value.reshape(value.shape[0], value.shape[1], -1)

    def my_rows(value):
        return lax.dynamic_slice_in_dim(value, mp_index * row_share, row_share, 1)

    def mine(value):
        return lax.dynamic_index_in_dim(value, mp_index, 0)

    positions = jnp.arange(length)
    self_valid = (
        (positions[None, :] <= positions[:, None])[None]
        & (positions[None, None, :] < target_len[:, None, None])
    )[:, None]
    mem_positions = jnp.arange(memory.shape[1])
    cross_valid = (mem_positions[None, :] < mine(memory_len)[:, None])[:, None, None, :]
    onehot = (
        jnp.asarray(bucket_table(length)).reshape(-1)[:, None] == jnp.arange(BUCKETS)[None, :]
    ).astype(jnp.float32)
    score_bias = (
        jnp.dot(onehot, pos_bias, precision=lax.Precision.HIGHEST)
        .reshape(length, length, heads_local)
        .transpose(2, 0, 1)[None]
    )
    cross_in = gather_mp(jnp.stack([query_cross, key_cross, value_cross]))
    cross_in = cross_in.transpose(1, 2, 0, 3).reshape(3, width, -1)
    cross_q, cross_k, cross_v = cross_in[0], cross_in[1], cross_in[2]
    cross_o = gather_mp(out_cross).reshape(-1, width)

    resid0 = targets.astype(jnp.float32)
    normed_one, inv_one = norm_forward(resid0, gain_self)
    normed_one = normed_one.astype(jnp.bfloat16)
    queries = split_heads(project(normed_one, query_self).astype(jnp.bfloat16))
    keys = split_heads(project(normed_one, key_self).astype(jnp.bfloat16))
    values = split_heads(project(normed_one, value_self).astype(jnp.bfloat16))
    mixed, log_one = attend(queries, keys, values, score_bias, self_valid)
    mixed = merge_heads(mixed).astype(jnp.bfloat16)
    resid1 = mine(resid0) + reduce_scatter(project(mixed, out_self), "mp", 0)

    mem_own = mine(memory)
    normed_two, inv_two = norm_forward(resid1, gain_cross)
    normed_two = normed_two.astype(jnp.bfloat16)
    queries_two = split_heads(project(normed_two, cross_q).astype(jnp.bfloat16))
    mem_keys = split_heads(project(mem_own, cross_k).astype(jnp.bfloat16))
    mem_values = split_heads(project(mem_own, cross_v).astype(jnp.bfloat16))
    mixed_two, log_two = attend(queries_two, mem_keys, mem_values, 0.0, cross_valid)
    mixed_two = merge_heads(mixed_two).astype(jnp.bfloat16)
    resid2 = resid1 + project(mixed_two, cross_o)
    normed_three, inv_three = norm_forward(resid2, gain_ffn)
    normed_all = gather_mp(normed_three.astype(jnp.bfloat16)[0])

    gate_pre = project(normed_all, gate_proj)
    up_pre = project(normed_all, up_proj)

    def gated(gate_in, up_in):
        return jax.nn.gelu(gate_in, approximate=True) * up_in

    hidden, hidden_pull = jax.vjp(gated, gate_pre, up_pre)
    hidden = hidden.astype(jnp.bfloat16)
    grad_gate_pre, grad_up_pre = hidden_pull(back_project(cotangent, down_proj))
    grad_gate_pre = grad_gate_pre.astype(jnp.bfloat16)
    grad_up_pre = grad_up_pre.astype(jnp.bfloat16)
    grad_normed = reduce_scatter(
        back_project(grad_gate_pre, gate_proj) + back_project(grad_up_pre, up_proj), "mp", 0
    )
    result = project(hidden, down_proj)
    own = (jnp.arange(targets.shape[0]) == mp_index)[:, None, None]
    result = result + jnp.where(own, resid2, 0.0)
    output = reduce_scatter(result, "mp", 1).astype(jnp.bfloat16)
    ffn_grads = jnp.concatenate(
        [
            weight_grad(normed_all, grad_gate_pre),
            weight_grad(normed_all, grad_up_pre),
            weight_grad(cotangent, hidden),
        ],
        1,
    )
    ffn_grads = reduce_scatter(ffn_grads, "dp", 0)
    grad_resid, grad_gain_ffn = norm_backward(resid2, inv_three, gain_ffn, grad_normed)
    grad_two = mine(cotangent).astype(jnp.float32) + grad_resid

    branch_two = grad_two.astype(jnp.bfloat16)
    grad_mixed_two = split_heads(back_project(branch_two, cross_o).astype(jnp.bfloat16))
    grad_q_two, grad_mem_keys, grad_mem_values, _ = attend_back(
        queries_two, mem_keys, mem_values, 0.0, cross_valid, log_two, grad_mixed_two
    )
    grad_q_two = merge_heads(grad_q_two).astype(jnp.bfloat16)
    grad_normed = back_project(grad_q_two, cross_q)
    grad_resid, grad_gain_cross = norm_backward(resid1, inv_two, gain_cross, grad_normed)
    grad_one = grad_two + grad_resid
    branch_one = gather_mp(grad_one.astype(jnp.bfloat16)[0])
    grad_mem_keys = merge_heads(grad_mem_keys).astype(jnp.bfloat16)
    grad_mem_values = merge_heads(grad_mem_values).astype(jnp.bfloat16)
    mem_grad = back_project(grad_mem_keys, cross_k) + back_project(grad_mem_values, cross_v)
    mem_rows = exchange_mp(mem_grad[0].astype(jnp.bfloat16))
    cross_grads = jnp.stack(
        [
            weight_grad(normed_two, grad_q_two),
            weight_grad(mem_own, grad_mem_keys),
            weight_grad(mem_own, grad_mem_values),
            weight_grad(branch_two, mixed_two),
        ],
        1,
    )
    cross_grads = reduce_scatter(cross_grads, "mp", 2)
    cross_grads = reduce_scatter(cross_grads, "dp", 0)

    grad_mixed = split_heads(back_project(branch_one, out_self).astype(jnp.bfloat16))
    grad_q_one, grad_k_one, grad_v_one, grad_scores = attend_back(
        queries, keys, values, score_bias, self_valid, log_one, grad_mixed
    )
    grad_q_one = merge_heads(grad_q_one).astype(jnp.bfloat16)
    grad_k_one = merge_heads(grad_k_one).astype(jnp.bfloat16)
    grad_v_one = merge_heads(grad_v_one).astype(jnp.bfloat16)
    score_total = jnp.sum(grad_scores.astype(jnp.float32), 0).reshape(heads_local, length * length)
    bias_local = jnp.dot(score_total, onehot, precision=lax.Precision.HIGHEST).T
    grad_normed = (
        back_project(grad_q_one, query_self)
        + back_project(grad_k_one, key_self)
        + back_project(grad_v_one, value_self)
    )
    gains = jnp.stack(
        [
            jnp.sum(grad_normed * (resid0 * inv_one), axis=(0, 1)),
            grad_gain_cross,
            grad_gain_ffn,
        ]
    )
    gains = sum_mp(gains)
    share = width // dp_size
    bias_columns = jnp.tile(bias_local.reshape(share, -1), (dp_size, 1))
    self_grads = jnp.concatenate(
        [
            weight_grad(normed_one, grad_q_one),
            weight_grad(normed_one, grad_k_one),
            weight_grad(normed_one, grad_v_one),
            weight_grad(branch_one, mixed),
            gains.T,
            bias_columns,
        ],
        1,
    )
    self_grads = reduce_scatter(self_grads, "dp", 0)
    grad_normed = reduce_scatter(grad_normed, "mp", 1)
    grad_resid, _ = norm_backward(my_rows(resid0), my_rows(inv_one), gain_self, grad_normed)
    grad_targets = (my_rows(branch_one).astype(jnp.float32) + grad_resid).astype(jnp.bfloat16)

    part = query_self.shape[1]
    units = gate_proj.shape[1]
    gains_at = 4 * part
    return (
        output,
        grad_targets,
        mem_rows,
        self_grads[:, :part],
        self_grads[:, part : 2 * part],
        self_grads[:, 2 * part : 3 * part],
        self_grads[:, 3 * part : 4 * part].T,
        cross_grads[:, 0],
        cross_grads[:, 1],
        cross_grads[:, 2],
        cross_grads[:, 3].T,
        ffn_grads[:, :units],
        ffn_grads[:, units : 2 * units],
        ffn_grads[:, 2 * units :].T,
        self_grads[:, gains_at],
        self_grads[:, gains_at + 1],
        self_grads[:, gains_at + 2],
        self_grads[:, gains_at + 3 :].reshape(bias_local.shape),
    )


def solution(mesh):
    fits = mesh.shape["dp"] == 8 and mesh.shape["mp"] == 4
    return jax.shard_map(
        on_device if fits else on_device_permutes,
        mesh=mesh,
        in_specs=(
            P("dp", None, None),
            P("dp", None, None),
            P("dp", None, None),
            P("dp"),
            P("dp"),
            P(None, "mp"),
            P(None, "mp"),
            P(None, "mp"),
            P("mp", None),
            P(None, "mp"),
            P(None, "mp"),
            P(None, "mp"),
            P("mp", None),
            P(None, "mp"),
            P(None, "mp"),
            P("mp", None),
            P(),
            P(),
            P(),
            P(None, "mp"),
        ),
        out_specs=(
            P("dp", "mp", None),
            P("dp", "mp", None),
            P("dp", "mp", None),
            P("dp", "mp"),
            P("dp", "mp"),
            P("dp", "mp"),
            P("mp", "dp"),
            P("dp", "mp"),
            P("dp", "mp"),
            P("dp", "mp"),
            P("mp", "dp"),
            P("dp", "mp"),
            P("dp", "mp"),
            P("mp", "dp"),
            P("dp"),
            P("dp"),
            P("dp"),
            P(None, "mp"),
        ),
        check_vma=False,
    )
```

profile of v0, /device:TPU:0, one launch (start us, length us, event | category | flops | bytes accessed | tf_op | source)
XLA Modules:
  0.0 193.7 jit_solution(12534272467090126117)
XLA Ops:
  0.7 0.0 copy-start
  0.7 2.0 %copy.39.wq_ref = bf16[768,192]{1,0:T(8,128)(2,1)} copy(bf16[768,192]{0,1:T(8,128)(2,1)} %param.26) | data formatting | bytes 589824 | tf_op args[5]
  2.7 1.9 copy.40.wk_ref
  4.6 0.9 copy.41.wv_ref
  5.5 0.0 copy-done.10
  5.5 0.9 copy.42.xq_hbm
  6.5 0.0 copy-done.11
  6.5 0.9 copy.43.xk_hbm
  7.4 0.9 copy.44.xv_hbm
  8.4 0.6 pad_maximum_fusion.gains_ref
  9.0 0.8 convolution_bitcast_fusion.dist_ref
  9.8 172.5 %layer.1 = (bf16[4,64,768]{2,1,0:T(8,128)(2,1)}, bf16[4,64,768]{2,1,0:T(8,128)(2,1)}, bf16[4,256,768]{2,1,0:T(8,128)(2,1)}, f32[3,96,512]{2,1,0:T(8,128)}, f32[3...) custom-call(s32[4]{0:T(128)} %tlen_ref.1, s32[4]{0:T(128)} %mlen_ref.1, bf16[4,256,768]{2,1,0:T(8,128)(2,1)} %x0_ref.1, ...), custom_call_target="tpu_custom_call" | custom-call | flops 24000000000 | bytes 16777216 | tf_op jit(solution)/shard_map/layer/pallas_call | solution.py:816
  182.4 1.4 copy-done.1
  183.8 1.1 copy-done.2
  184.8 1.0 copy-done.4
  185.8 1.0 copy-done.5
  186.8 1.0 copy-done.6
  187.8 1.0 copy-done.7
  188.7 0.8 copy-done.8
  189.5 2.1 %finish.1 = (bf16[4,64,768]{2,1,0:T(8,128)(2,1)}, bf16[4,64,768]{2,1,0:T(8,128)(2,1)}, bf16[4,256,768]{2,1,0:T(8,128)(2,1)}, f32[96,192]{1,0:T(8,128)}, f32[96,1...) custom-call(f32[3,96,512]{2,1,0:T(8,128)S(1)} %copy-done.2, ...), custom_call_target="tpu_custom_call" | custom-call | tf_op jit(solution)/shard_map/finish/pallas_call | solution.py:844
  191.7 0.1 constant_dynamic-slice_fusion
  191.7 0.5 slice_bitcast_fusion
  192.3 0.8 copy.45
  193.1 0.7 copy.46
  (26 shorter events, 0.1 us)
Async XLA Ops:
  0.7 8.3 %copy-start = (f32[32,3]{0,1:T(4,128)S(1)}, f32[32,3]{0,1:T(4,128)}, u32[]{:S(2)}) copy-start(f32[32,3]{0,1:T(4,128)} %param.40) | copy-start | bytes 1156
  0.7 3.9 %copy-start.9 = (bf16[768,192]{0,1:T(8,128)(2,1)S(1)}, bf16[768,192]{0,1:T(8,128)(2,1)}, u32[]{:S(2)}) copy-start(bf16[768,192]{0,1:T(8,128)(2,1)} %param.28) | copy-start | bytes 884740
  0.7 4.9 %copy-start.10 = (bf16[768,192]{0,1:T(8,128)(2,1)S(1)}, bf16[768,192]{0,1:T(8,128)(2,1)}, u32[]{:S(2)}) copy-start(bf16[768,192]{0,1:T(8,128)(2,1)} %param.30) | copy-start | bytes 884740
  0.7 5.8 %copy-start.11 = (bf16[768,192]{0,1:T(8,128)(2,1)S(1)}, bf16[768,192]{0,1:T(8,128)(2,1)}, u32[]{:S(2)}) copy-start(bf16[768,192]{0,1:T(8,128)(2,1)} %param.31) | copy-start | bytes 884740
  0.7 6.7 %copy-start.12 = (bf16[768,192]{0,1:T(8,128)(2,1)S(1)}, bf16[768,192]{0,1:T(8,128)(2,1)}, u32[]{:S(2)}) copy-start(bf16[768,192]{0,1:T(8,128)(2,1)} %param.32) | copy-start | bytes 884740
  2.7 5.6 %copy-start.13 = (f32[768]{0:T(1024)S(1)}, f32[768]{0:T(1024)}, u32[]{:S(2)}) copy-start(f32[768]{0:T(1024)} %param.37) | copy-start | bytes 9220
  2.7 5.6 %copy-start.14 = (f32[768]{0:T(1024)S(1)}, f32[768]{0:T(1024)}, u32[]{:S(2)}) copy-start(f32[768]{0:T(1024)} %param.38) | copy-start | bytes 9220
  2.7 5.7 %copy-start.15 = (f32[768]{0:T(1024)S(1)}, f32[768]{0:T(1024)}, u32[]{:S(2)}) copy-start(f32[768]{0:T(1024)} %param.39) | copy-start | bytes 9220
  2.7 6.3 %copy-start.3 = (f32[256,32]{1,0:T(8,128)S(1)}, f32[256,32]{1,0:T(8,128)}, u32[]{:S(2)}) copy-start(f32[256,32]{1,0:T(8,128)} %constant.12.clone.onehot_ref) | copy-start | bytes 98308
  182.3 1.4 copy-start.1
  183.8 1.1 copy-start.2
  184.8 1.0 copy-start.4
  185.8 1.0 copy-start.5
  186.8 1.0 copy-start.6
  187.8 1.0 copy-start.7
  188.7 0.8 copy-start.8
where the time goes:
time: 194 us
  Pallas kernels  175 us (90%)
  local copies, waits for them, and re-layouts  16.9 us (9%)
    pallas_call x1, Pallas kernels, on_device(): pl.pallas_call(layer_kernel, out_shape=[rows, rows, struct((seqs, slots /...  173 us
    unnamed x40, local copies, waits for them, and re-layouts  16.2 us

commit v1 on v0

--- a/solution.py
+++ b/solution.py
@@ -27,7 +27,7 @@
 F32 = jnp.float32
 BF16 = jnp.bfloat16
 CHUNK = 256
-COPIES = 64
+COPIES = 120
 
 
 def dot(left, right, left_dim, right_dim):
@@ -60,13 +60,27 @@
     return grad_resid, jnp.sum(grad * unit, 0, keepdims=True)
 
 
+def bucket_ranges(length):
+    of_distance = bucket_table(length)[:, 0]
+    ranges = []
+    for k in range(BUCKETS):
+        inside = np.flatnonzero(of_distance == k)
+        ranges.append((int(inside[0]), int(inside[-1]) + 1) if len(inside) else (0, 0))
+    return ranges
+
+
+def place_of(chunk, order):
+    y, z1, z2 = chunk % 2, chunk // 2 % 2, chunk // 4
+    return 4 * y + 2 * z1 + z2 if order == "y" else 4 * z1 + 2 * y + z2
+
+
 def layer_kernel(
-    tlen_ref, mlen_ref, x0_ref, wq_ref, wk_ref, wv_ref, wo_ref, gains_ref, dist_ref,
-    mem_hbm, cot_hbm, xq_hbm, xk_hbm, xv_hbm, xo_hbm, wg_hbm, wu_hbm, wd_hbm,
+    tlen_ref, mlen_ref, pos_ref, gain_self_ref, gain_cross_ref, gain_ffn_ref,
+    x0_hbm, wq_hbm, wk_hbm, wv_hbm, wo_hbm, mem_hbm, cot_hbm, xq_hbm, xk_hbm, xv_hbm, xo_hbm, wg_hbm, wu_hbm, wd_hbm,
     out_ref, gt_ref, gm_ref, gf_ref, gx_ref, gs_ref, small_ref,
     q1, k1, v1, e1, r1, u1, o1, bias,
     part_send, part_recv, dn_recv, acc,
-    mem, cot, wg, wu, wd, cross_w,
+    x0_ref, wq_ref, wk_ref, wv_ref, wo_ref, mem, cot, wg, wu, wd, cross_w,
     x1, x2, n2, q2, kv2, e2, r2, u2, o2,
     n3, units, rows_low, rows_recv, rows_send_x, rows_recv_x,
     c2, turned, c1, f_low, f_recv0, f_recv1, f_recv2,
@@ -82,21 +96,28 @@
     across = 2 * other_chip + other_core
     at_dp = lax.axis_index("dp")
     bit_y, bit_z1, bit_z2 = lax.rem(at_dp, 2), lax.rem(lax.div(at_dp, 2), 2), lax.div(at_dp, 4)
-    by_y = at_dp + 1 - 2 * bit_y
-    by_z1 = at_dp + 2 - 4 * bit_z1
-    by_z2 = at_dp + 4 - 8 * bit_z2
     to_core, to_x, to_across = {"mp": by_core}, {"mp": by_x}, {"mp": across}
-    to_y, to_z1, to_z2 = {"dp": by_y}, {"dp": by_z1}, {"dp": by_z2}
+    to_y = {"dp": at_dp + 1 - 2 * bit_y}
+    to_z1 = {"dp": at_dp + 2 - 4 * bit_z1}
+    to_z2 = {"dp": at_dp + 4 - 8 * bit_z2}
 
     seqs, length, width = x0_ref.shape
-    part = wq_ref.shape[1]
+    part = wq_ref.shape[0]
     heads = part // HEAD_DIM
     slots = mem.shape[0]
     blocks = cross_w.shape[0]
     share = width // 8
     quarter = length // blocks
-
+    half = length // 2
+
+    gain_self_row, gain_cross_row, gain_ffn_row = (
+        ref[...].reshape(1, width) for ref in (gain_self_ref, gain_cross_ref, gain_ffn_ref)
+    )
     sent = {}
+    names = iter(range(COPIES))
+
+    def fresh(count):
+        return [next(names) for _ in range(count)]
 
     def remote(i, src, dst, device):
         return pltpu.make_async_remote_copy(
@@ -104,17 +125,72 @@
             device_id=device, device_id_type=pl.DeviceIdType.MESH,
         )
 
+    def note(i, src, dst, device, waited=False):
+        sent[i] = remote(i, src, dst, device)
+
     def send(i, src, dst, device):
-        copy = remote(i, src, dst, device)
-        copy.start()
-        sent[i] = copy
-
-    def left(*names):
-        for name in names:
-            sent.pop(name).wait_send()
+        remote(i, src, dst, device).start()
+        note(i, src, dst, device)
+
+    def left(*sends):
+        for i in sends:
+            sent.pop(i).wait_send()
 
     def arrived(i, dst, device):
         remote(i, dst, dst, device).wait_recv()
+
+    def add_rows(ref, at, recv, from_at):
+        ref[at, :] = (ref[at, :].astype(F32) + recv[from_at, :].astype(F32)).astype(BF16)
+
+    class Sum:
+        def __init__(self, low, recvs, order):
+            self.low, self.recvs = low, recvs
+            bits = (bit_y, bit_z1, bit_z2) if order == "y" else (bit_z1, bit_y, bit_z2)
+            self.devices = (to_y, to_z1, to_z2) if order == "y" else (to_z1, to_y, to_z2)
+            self.ids = fresh(3)
+            self.away, self.kept, self.away_in, self.kept_in = [], [], [], []
+            base = 0
+            for k, bit in enumerate(bits):
+                count = (4 >> k) * share
+
+                def rows(start):
+                    return pl.ds(pl.multiple_of(start, share), count)
+
+                self.away.append(rows(base + (1 - bit) * count))
+                self.kept.append(rows(base + bit * count))
+                self.away_in.append(rows((1 - bit) * count))
+                self.kept_in.append(rows(bit * count))
+                base = base + bit * count
+
+        def copy(self, k):
+            return (self.ids[k], self.low.at[self.away[k]], self.recvs[k], self.devices[k])
+
+        def start(self):
+            send(*self.copy(0))
+
+        def start_with(self, landed):
+            add_rows(self.low, self.away[0], landed, self.away[0])
+            send(*self.copy(0))
+            add_rows(self.low, self.kept[0], landed, self.kept[0])
+
+        def step(self, k, in_loop=False):
+            recv = self.recvs[k - 1]
+            arrived(self.ids[k - 1], recv, self.devices[k - 1])
+            add_rows(self.low, self.away[k], recv, self.away_in[k])
+            if in_loop:
+                remote(*self.copy(k)).start()
+            else:
+                send(*self.copy(k))
+            add_rows(self.low, self.kept[k], recv, self.kept_in[k])
+
+        def total(self):
+            arrived(self.ids[2], self.recvs[2], self.devices[2])
+            return self.low[self.kept[2], :].astype(F32) + self.recvs[2][...].astype(F32)
+
+    def neighbour(t):
+        flip_x, flip_core = lax.div(t, 2), lax.rem(t, 2)
+        at_x = chip + flip_x * (other_chip - chip)
+        return 2 * at_x + core + flip_core * (other_core - core)
 
     barrier = pltpu.get_barrier_semaphore()
     partners = (to_core, to_x, to_across, to_y, to_z1, to_z2)
@@ -122,56 +198,120 @@
         pl.semaphore_signal(barrier, inc=1, device_id=device, device_id_type=pl.DeviceIdType.MESH)
 
     loads = [
-        pltpu.make_async_copy(xo_hbm, cross_w.at[me, 3 * part : 4 * part], local_sem.at[3]),
-        pltpu.make_async_copy(mem_hbm.at[me], mem, local_sem.at[4]),
-        pltpu.make_async_copy(cot_hbm, cot, local_sem.at[5]),
-        pltpu.make_async_copy(wg_hbm, wg, local_sem.at[6]),
-        pltpu.make_async_copy(wu_hbm, wu, local_sem.at[7]),
-        pltpu.make_async_copy(wd_hbm, wd, local_sem.at[8]),
+        pltpu.make_async_copy(source, target, local_sem.at[i])
+        for i, (source, target) in enumerate((
+            (xk_hbm, cross_w.at[me, 0:part]),
+            (xv_hbm, cross_w.at[me, part : 2 * part]),
+            (xq_hbm, cross_w.at[me, 2 * part : 3 * part]),
+            (xo_hbm, cross_w.at[me, 3 * part : 4 * part]),
+            (x0_hbm, x0_ref),
+            (wq_hbm, wq_ref),
+            (wk_hbm, wk_ref),
+            (wv_hbm, wv_ref),
+            (wo_hbm, wo_ref),
+            (mem_hbm.at[me], mem),
+            (cot_hbm, cot),
+            (wg_hbm, wg),
+            (wu_hbm, wu),
+            (wd_hbm, wd),
+        ))
     ]
-    staged = [
-        pltpu.make_async_copy(
-            source.at[i * CHUNK : (i + 1) * CHUNK], stage.at[i], local_sem.at[10 + 3 * j + i]
-        )
-        for j, (source, stage) in enumerate(((xk_hbm, k1), (xv_hbm, v1), (xq_hbm, q1)))
-        for i in range(width // CHUNK)
-    ]
-    for load in staged + loads:
+    for load in loads[:9]:
+        load.start()
+    for load in loads[:4]:
+        load.wait()
+    pl.semaphore_wait(barrier, len(partners))
+
+    def piece(flip_y, flip_z1, p):
+        at_y = bit_y + flip_y * (1 - 2 * bit_y)
+        at_z1 = bit_z1 + flip_z1 * (1 - 2 * bit_z1)
+        start = part * (at_y + 2 * at_z1) + share * p
+        return pl.ds(pl.multiple_of(start, share), share)
+
+    lows, highs = slice(0, 2 * part), slice(2 * part, 4 * part)
+    w_core, w_x, w_y, w_z1, w_on = fresh(2), fresh(2), fresh(3), fresh(3), fresh(8)
+
+    def weights_on(i, rows, device, in_loop=False):
+        copy = (i, cross_w.at[by_x, rows], cross_w.at[by_x, rows], device)
+        if in_loop:
+            remote(*copy).start()
+        else:
+            send(*copy)
+        return copy
+
+    def weights_from(i, rows, device):
+        arrived(i, cross_w.at[by_x, rows], device)
+
+    def weights_from_x(p, in_loop=False):
+        rows = piece(0, 0, p)
+        weights_from(w_x[p], rows, to_x)
+        return [
+            weights_on(w_y[p], rows, to_y, in_loop),
+            weights_on(w_z1[p], rows, to_z1, in_loop),
+            weights_on(w_on[p], rows, to_core, in_loop),
+        ]
+
+    def weights_near(p):
+        from_y, from_z1 = piece(1, 0, p), piece(0, 1, p)
+        weights_from(w_y[p], from_y, to_y)
+        if p == 0:
+            weights_on(w_z1[2], from_y, to_z1)
+        weights_on(w_on[2 + p], from_y, to_core)
+        weights_from(w_z1[p], from_z1, to_z1)
+        if p == 1:
+            weights_on(w_y[2], from_z1, to_y)
+        weights_on(w_on[4 + p], from_z1, to_core)
+
+    def weights_far():
+        weights_from(w_z1[2], piece(1, 1, 0), to_z1)
+        weights_on(w_on[6], piece(1, 1, 0), to_core)
+        weights_from(w_y[2], piece(1, 1, 1), to_y)
+        weights_on(w_on[7], piece(1, 1, 1), to_core)
+
+    def weights_from_core():
+        for i, (flip_y, flip_z1) in enumerate(((0, 0), (1, 0), (0, 1), (1, 1))):
+            for p in range(2):
+                rows = piece(flip_y, flip_z1, p)
+                arrived(w_on[2 * i + p], cross_w.at[across, rows], to_core)
+
+    for p in range(2):
+        rows = piece(0, 0, p)
+        send(w_x[p], cross_w.at[me, rows], cross_w.at[me, rows], to_x)
+    send(w_core[0], cross_w.at[me, lows], cross_w.at[me, lows], to_core)
+    send(w_core[1], cross_w.at[me, highs], cross_w.at[me, highs], to_core)
+    for load in loads[9:]:
         load.start()
 
     key_at = lax.broadcasted_iota(jnp.int32, (length, length), 0)
     query_at = lax.broadcasted_iota(jnp.int32, (length, length), 1)
+    distance = lax.broadcasted_iota(jnp.int32, (8, length), 1)
     for h in range(heads):
-        spread = jnp.broadcast_to(dist_ref[h : h + 1, :], (length, length))
+        of_distance = jnp.zeros((8, length), F32)
+        for k, (first, last) in enumerate(bucket_ranges(length)):
+            inside = (distance >= first) & (distance < last)
+            of_distance = jnp.where(inside, pos_ref[h, k], of_distance)
+        spread = jnp.broadcast_to(of_distance[0:1], (length, length))
         shifted = pltpu.roll(spread, 0, 1, stride=1, stride_axis=0)
         bias[h] = jnp.where(key_at <= query_at, shifted, NEG)
 
-    for load in staged:
+    for load in loads[4:9]:
         load.wait()
-    for j, stage in enumerate((k1, v1, q1)):
-        for i in range(width // CHUNK):
-            cols = slice(i * CHUNK, (i + 1) * CHUNK)
-            cross_w[me, j * part : (j + 1) * part, cols] = stage[i].T
-    loads[0].wait()
-    pl.semaphore_wait(barrier, len(partners))
-
-    lows, highs = slice(0, 2 * part), slice(2 * part, 4 * part)
-    send(0, cross_w.at[me, lows], cross_w.at[me, lows], to_x)
-    send(1, cross_w.at[me, lows], cross_w.at[me, lows], to_core)
-    send(2, cross_w.at[me, highs], cross_w.at[me, highs], to_x)
-    send(3, cross_w.at[me, highs], cross_w.at[me, highs], to_core)
+
+    x1_core0, x1_x, x1_core1 = fresh(3)
 
     def self_one(t, carry):
-        flip_x, flip_core = 1 - lax.div(t, 2), 1 - lax.rem(t, 2)
-        at_x = chip + flip_x - 2 * chip * flip_x
-        at_core = core + flip_core - 2 * core * flip_core
-        s = 2 * at_x + at_core
+        s = neighbour(3 - t)
+
+        @pl.when(t == 3)
+        def _():
+            weights_from_x(0, True)
+
         resid = x0_ref[s].astype(F32)
         _, unit = unit_rows(resid)
-        n = (unit * gains_ref[0:1, :]).astype(BF16)
-        q = dot_nn(n, wq_ref[...]).astype(BF16)
-        k = dot_nn(n, wk_ref[...]).astype(BF16)
-        v = dot_nn(n, wv_ref[...]).astype(BF16)
+        n = (unit * gain_self_row).astype(BF16)
+        q = dot_nt(n, wq_ref[...]).astype(BF16)
+        k = dot_nt(n, wk_ref[...]).astype(BF16)
+        v = dot_nt(n, wv_ref[...]).astype(BF16)
         q1[s], k1[s], v1[s] = q, k, v
         mixed = []
         for h in range(heads):
@@ -193,18 +333,18 @@
         @pl.when(t == 0)
         def _():
             part_send[0] = value.astype(BF16)
-            remote(4, part_send.at[0], part_recv.at[0], to_core).start()
+            remote(x1_core0, part_send.at[0], part_recv.at[0], to_core).start()
 
         @pl.when(t == 1)
         def _():
-            arrived(4, part_recv.at[0], to_core)
+            arrived(x1_core0, part_recv.at[0], to_core)
             part_send[1] = (value + part_recv[0].astype(F32)).astype(BF16)
-            remote(5, part_send.at[1], part_recv.at[1], to_x).start()
+            remote(x1_x, part_send.at[1], part_recv.at[1], to_x).start()
 
         @pl.when(t == 2)
         def _():
             part_send[2] = value.astype(BF16)
-            remote(6, part_send.at[2], part_recv.at[2], to_core).start()
+            remote(x1_core1, part_send.at[2], part_recv.at[2], to_core).start()
 
         @pl.when(t == 3)
         def _():
@@ -213,42 +353,58 @@
         return carry
 
     lax.fori_loop(0, seqs, self_one, 0)
-    sent[4] = remote(4, part_send.at[0], part_recv.at[0], to_core)
-    sent[5] = remote(5, part_send.at[1], part_recv.at[1], to_x)
-    sent[6] = remote(6, part_send.at[2], part_recv.at[2], to_core)
-
-    arrived(0, cross_w.at[by_x, lows], to_x)
-    send(7, cross_w.at[by_x, lows], cross_w.at[by_x, lows], to_core)
-    arrived(1, cross_w.at[by_core, lows], to_core)
-    arrived(7, cross_w.at[across, lows], to_core)
-    loads[1].wait()
-
-    def keys_values(b, carry):
+    note(x1_core0, part_send.at[0], part_recv.at[0], to_core, waited=True)
+    note(x1_x, part_send.at[1], part_recv.at[1], to_x)
+    note(x1_core1, part_send.at[2], part_recv.at[2], to_core)
+
+    first = piece(0, 0, 0)
+    for i, device in ((w_y[0], to_y), (w_z1[0], to_z1), (w_on[0], to_core)):
+        note(i, cross_w.at[by_x, first], cross_w.at[by_x, first], device)
+
+    def keys_values(b):
         for at in range(0, slots, CHUNK):
             rows = slice(at, at + CHUNK)
             kv2[b, rows, :] = dot_nt(mem[rows, :], cross_w[b, lows, :]).astype(BF16)
+
+    loads[9].wait()
+    arrived(w_core[0], cross_w.at[by_core, lows], to_core)
+
+    def near_keys(t, carry):
+        keys_values(neighbour(t))
         return carry
 
-    lax.fori_loop(0, blocks, keys_values, 0)
-    arrived(2, cross_w.at[by_x, highs], to_x)
-    send(8, cross_w.at[by_x, highs], cross_w.at[by_x, highs], to_core)
-    arrived(3, cross_w.at[by_core, highs], to_core)
-    arrived(6, part_recv.at[2], to_core)
-    arrived(5, part_recv.at[1], to_x)
+    lax.fori_loop(0, 2, near_keys, 0)
+    weights_from_x(1)
+    weights_near(0)
+    arrived(w_core[1], cross_w.at[by_core, highs], to_core)
+    weights_near(1)
+    arrived(x1_core1, part_recv.at[2], to_core)
+    arrived(x1_x, part_recv.at[1], to_x)
 
     def enter_cross(i, carry):
         rows = pl.ds(pl.multiple_of(i * quarter, quarter), quarter)
         resid = x1[rows, :] + part_recv[1, rows, :].astype(F32) + part_recv[2, rows, :].astype(F32)
         x1[rows, :] = resid
         x2[rows, :] = resid
-        n2[rows, :] = (unit_rows(resid)[1] * gains_ref[1:2, :]).astype(BF16)
+        n2[rows, :] = (unit_rows(resid)[1] * gain_cross_row).astype(BF16)
         return carry
 
     lax.fori_loop(0, blocks, enter_cross, 0)
-    arrived(8, cross_w.at[across, highs], to_core)
+    weights_far()
     slot_at = lax.broadcasted_iota(jnp.int32, (CHUNK, length), 0)
 
-    def cross_one(b, carry):
+    def cross_one(t, carry):
+        b = neighbour(t)
+
+        @pl.when(t == 2)
+        def _():
+            keys_values(by_x)
+
+        @pl.when(t == 3)
+        def _():
+            weights_from_core()
+            keys_values(across)
+
         q = dot_nt(n2[...], cross_w[b, 2 * part : 3 * part, :]).astype(BF16)
         q2[b] = q
         mixed = []
@@ -283,40 +439,81 @@
 
     lax.fori_loop(0, blocks, cross_one, 0)
 
+    n3_x, n3_core, n3_on = fresh(2), next(names), fresh(2)
+    dn_near, dn_core, dn_x = next(names), fresh(2), fresh(2)
+    halves = [slice(0, half), slice(half, length)]
+
     def enter_ffn(i, carry):
         rows = pl.ds(pl.multiple_of(i * quarter, quarter), quarter)
-        n3[me, rows, :] = (unit_rows(x2[rows, :])[1] * gains_ref[2:3, :]).astype(BF16)
+        n3[me, rows, :] = (unit_rows(x2[rows, :])[1] * gain_ffn_row).astype(BF16)
         return carry
 
-    lax.fori_loop(0, blocks, enter_ffn, 0)
-    send(9, n3.at[me], n3.at[me], to_x)
-    send(10, n3.at[me], n3.at[me], to_core)
-    for load in loads[2:]:
+    for i in range(2):
+        lax.fori_loop(2 * i, 2 * i + 2, enter_ffn, 0)
+        send(n3_x[i], n3.at[me, halves[i]], n3.at[me, halves[i]], to_x)
+    send(n3_core, n3.at[me], n3.at[me], to_core)
+    for load in loads[10:]:
         load.wait()
-    left(4, 5, 6)
+    left(x1_core0, x1_x, x1_core1)
     scale, cubic = 0.7978845608028654, 0.044715
 
+    def turn(slot, value, first_col, order=None):
+        value = value.T
+        cols = pl.ds(first_col, value.shape[1])
+        if order is None:
+            turned[slot, :, cols] = value
+            return
+        for j in range(8):
+            at = place_of(j, order) * share
+            turned[slot, at : at + share, cols] = value[j * share : (j + 1) * share]
+
+    def turn_normed(s):
+        turn(0, n3[s], pl.multiple_of(s * length, length), "y")
+
+    def pass_dn(i):
+        arrived(dn_core[i], dn_recv.at[1, halves[i]], to_core)
+        part_send[2, halves[i], :] = (
+            part_send[2, halves[i], :].astype(F32) + dn_recv[1, halves[i], :].astype(F32)
+        ).astype(BF16)
+        remote(dn_x[i], part_send.at[2, halves[i]], dn_recv.at[2, halves[i]], to_x).start()
+
     def ffn_one(t, carry):
-        flip_x, flip_core = lax.div(t, 2), lax.rem(t, 2)
-        at_x = chip + flip_x - 2 * chip * flip_x
-        at_core = core + flip_core - 2 * core * flip_core
-        s = 2 * at_x + at_core
+        late, odd = lax.div(t, 2), lax.rem(t, 2)
+        at_x = chip + late * (other_chip - chip)
+        near_core = (1 - late) * odd
+        seq_a = 2 * at_x + core + near_core * (other_core - core)
+        seq_b = 2 * at_x + core + (late + near_core) * (other_core - core)
+        half_a, half_b = late * odd, 1 - late + late * odd
+        in_a = pl.ds(pl.multiple_of(half_a * half, half), half)
+        in_b = pl.ds(pl.multiple_of(half_b * half, half), half)
+        rows_a = pl.ds(pl.multiple_of(seq_a * length + half_a * half, half), half)
+        rows_b = pl.ds(pl.multiple_of(seq_b * length + half_b * half, half), half)
 
         @pl.when(t == 1)
         def _():
-            arrived(10, n3.at[by_core], to_core)
+            arrived(n3_core, n3.at[by_core], to_core)
 
         @pl.when(t == 2)
         def _():
-            arrived(9, n3.at[by_x], to_x)
-            remote(11, n3.at[by_x], n3.at[by_x], to_core).start()
+            turn_normed(me)
+            turn_normed(by_core)
+            arrived(n3_x[0], n3.at[by_x, halves[0]], to_x)
+            remote(n3_on[0], n3.at[by_x, halves[0]], n3.at[by_x, halves[0]], to_core).start()
+            turn(1, cot[0], 0, "z1")
+            turn(1, cot[1], length, "z1")
+            arrived(n3_on[0], n3.at[across, halves[0]], to_core)
 
         @pl.when(t == 3)
         def _():
-            arrived(11, n3.at[across], to_core)
-
-        n, c = n3[s], cot[s]
-        rows = pl.ds(pl.multiple_of(s * length, length), length)
+            pass_dn(0)
+            arrived(n3_x[1], n3.at[by_x, halves[1]], to_x)
+            remote(n3_on[1], n3.at[by_x, halves[1]], n3.at[by_x, halves[1]], to_core).start()
+            turn(1, cot[2], 2 * length, "z1")
+            turn(1, cot[3], 3 * length, "z1")
+            arrived(n3_on[1], n3.at[across, halves[1]], to_core)
+
+        n = jnp.concatenate([n3[seq_a, in_a, :], n3[seq_b, in_b, :]], 0)
+        c = jnp.concatenate([cot[seq_a, in_a, :], cot[seq_b, in_b, :]], 0)
         for at in range(0, wg.shape[1], CHUNK):
             cols = slice(at, at + CHUNK)
             a = dot_nn(n, wg[:, cols])
@@ -324,13 +521,18 @@
             dh = dot_nt(c, wd[cols, :])
             square = a * a
             slope = jnp.tanh(scale * (a + cubic * (a * square)))
-            half = 0.5 * (1.0 + slope)
-            gelu = a * half
-            rise = half + 0.5 * a * (1.0 - slope * slope) * (scale * (1.0 + 3.0 * cubic * square))
-            units[0, rows, cols] = (dh * b * rise).astype(BF16)
-            units[1, rows, cols] = (dh * gelu).astype(BF16)
-            units[2, rows, cols] = (gelu * b).astype(BF16)
-        dn = dot_nt(units[0, rows, :], wg[...]) + dot_nt(units[1, rows, :], wu[...])
+            mid = 0.5 * (1.0 + slope)
+            gelu = a * mid
+            rise = mid + 0.5 * a * (1.0 - slope * slope) * (scale * (1.0 + 3.0 * cubic * square))
+            for i, value in enumerate((dh * b * rise, dh * gelu, gelu * b)):
+                value = value.astype(BF16)
+                units[i, rows_a, cols] = value[:half]
+                units[i, rows_b, cols] = value[half:]
+
+        def both(i):
+            return jnp.concatenate([units[i, rows_a, :], units[i, rows_b, :]], 0)
+
+        dn = dot_nt(both(0), wg[...]) + dot_nt(both(1), wu[...])
 
         @pl.when(t == 0)
         def _():
@@ -339,70 +541,68 @@
         @pl.when(t == 1)
         def _():
             part_send[0] = dn.astype(BF16)
-            remote(12, part_send.at[0], dn_recv.at[0], to_core).start()
-
-        @pl.when(t == 2)
-        def _():
-            part_send[2] = dn.astype(BF16)
-
-        @pl.when(t == 3)
-        def _():
-            part_send[1] = dn.astype(BF16)
-            remote(13, part_send.at[1], dn_recv.at[1], to_core).start()
+            remote(dn_near, part_send.at[0], dn_recv.at[0], to_core).start()
+
+        for i in range(2):
+
+            @pl.when(t == 2 + i)
+            def _(i=i):
+                part_send[1, halves[i], :] = dn[half:].astype(BF16)
+                remote(
+                    dn_core[i], part_send.at[1, halves[i]], dn_recv.at[1, halves[i]], to_core
+                ).start()
+                part_send[2, halves[i], :] = dn[:half].astype(BF16)
 
         own = jnp.where(t == 0, 1.0, 0.0)
-        result = dot_nn(units[2, rows, :], wd[...]) + own * x2[...]
-        for i in range(blocks):
-            rows_low[i % 2, i // 2, s] = result[i * quarter : (i + 1) * quarter].astype(BF16)
+        result = (dot_nn(both(2), wd[...]) + own * x2[...]).astype(BF16)
+        rows_low[0, half_a, seq_a] = result[0:quarter]
+        rows_low[1, half_a, seq_a] = result[quarter : 2 * quarter]
+        rows_low[0, half_b, seq_b] = result[2 * quarter : 3 * quarter]
+        rows_low[1, half_b, seq_b] = result[3 * quarter :]
         return carry
 
     lax.fori_loop(0, seqs, ffn_one, 0)
-    sent[11] = remote(11, n3.at[by_x], n3.at[by_x], to_core)
-    arrived(13, dn_recv.at[1], to_core)
-    part_send[2] = (part_send[2].astype(F32) + dn_recv[1].astype(F32)).astype(BF16)
-    send(14, part_send.at[2], dn_recv.at[2], to_x)
-    sent[12] = remote(12, part_send.at[0], dn_recv.at[0], to_core)
-    sent[13] = remote(13, part_send.at[1], dn_recv.at[1], to_core)
-    send(15, rows_low.at[other_core], rows_recv, to_core)
-
-    def turn(slot, value, first_col, order):
-        value = value.T
-        for j in range(8):
-            y, z1, z2 = j % 2, j // 2 % 2, j // 4
-            at = (4 * y + 2 * z1 + z2) if order == "y" else (4 * z1 + 2 * y + z2)
-            cols = slice(first_col, first_col + value.shape[1])
-            turned[slot, at * share : (at + 1) * share, cols] = value[j * share : (j + 1) * share]
-
-    for s in range(seqs):
-        turn(0, n3[s], s * length, "y")
-        turn(1, cot[s], s * length, "y")
-
-    half_rows = 4 * share
-
-    def half_at(bit):
-        return pl.ds(pl.multiple_of(bit * half_rows, half_rows), half_rows)
-
-    for keep in (False, True):
-        for i in range(3):
-            rows = half_at(bit_y if keep else 1 - bit_y)
-            f_low[i, rows, :] = dot_nn(turned[i // 2, rows, :], units[i]).astype(BF16)
-            if not keep:
-                send(16 + i, f_low.at[i, rows], f_recv0.at[i], to_y)
-
-    arrived(15, rows_recv, to_core)
+    pass_dn(1)
+    for i in range(2):
+        note(n3_on[i], n3.at[by_x, halves[i]], n3.at[by_x, halves[i]], to_core, waited=True)
+        note(
+            dn_core[i], part_send.at[1, halves[i]], dn_recv.at[1, halves[i]], to_core, waited=True
+        )
+        note(dn_x[i], part_send.at[2, halves[i]], dn_recv.at[2, halves[i]], to_x)
+    note(dn_near, part_send.at[0], dn_recv.at[0], to_core)
+    out_core, out_x = fresh(2)
+    send(out_core, rows_low.at[other_core], rows_recv, to_core)
+    turn_normed(by_x)
+    turn_normed(across)
+    orders = ("y", "y", "z1")
+    f_sums = [
+        Sum(f_low.at[i], [f_recv0.at[i], f_recv1.at[i], f_recv2.at[i]], orders[i]) for i in range(3)
+    ]
+
+    def ffn_grad(i, rows):
+        f_low[i, rows, :] = dot_nn(turned[i // 2, rows, :], units[i]).astype(BF16)
+
+    for i in (0, 2, 1):
+        ffn_grad(i, f_sums[i].away[0])
+        f_sums[i].start()
+    for i in (0, 2, 1):
+        ffn_grad(i, f_sums[i].kept[0])
+
+    arrived(out_core, rows_recv, to_core)
     rows_send_x[...] = (
         rows_low[core, other_chip].astype(F32) + rows_recv[other_chip].astype(F32)
     ).astype(BF16)
-    send(19, rows_send_x, rows_recv_x, to_x)
-
-    arrived(12, dn_recv.at[0], to_core)
-    arrived(14, dn_recv.at[2], to_x)
+    send(out_x, rows_send_x, rows_recv_x, to_x)
+
+    arrived(dn_near, dn_recv.at[0], to_core)
+    for i in range(2):
+        arrived(dn_x[i], dn_recv.at[2, halves[i]], to_x)
     small[...] = jnp.zeros_like(small)
 
     def enter_back(i, carry):
         rows = pl.ds(pl.multiple_of(i * quarter, quarter), quarter)
         dn3 = acc[rows, :] + dn_recv[0, rows, :].astype(F32) + dn_recv[2, rows, :].astype(F32)
-        grad, gain_ffn = norm_back(x2[rows, :], gains_ref[2:3, :], dn3)
+        grad, gain_ffn = norm_back(x2[rows, :], gain_ffn_row, dn3)
         dx2 = cot[me, rows, :].astype(F32) + grad
         acc[rows, :] = dx2
         c2[rows, :] = dx2.astype(BF16)
@@ -412,6 +612,11 @@
     lax.fori_loop(0, blocks, enter_back, 0)
 
     def cross_back(b, carry):
+        @pl.when(b == 3)
+        def _():
+            f_sums[0].step(1, True)
+            f_sums[2].step(1, True)
+
         do = dot_nt(cross_w[b, 3 * part : 4 * part, :], c2[...])
         q = q2[b]
         dqs = []
@@ -435,6 +640,8 @@
         return carry
 
     lax.fori_loop(0, blocks, cross_back, 0)
+    for i in (0, 2):
+        note(*f_sums[i].copy(1))
     dn2 = dot_nn(q2[0], cross_w[0, 2 * part : 3 * part, :])
     for b in range(1, blocks):
         dn2 = dn2 + dot_nn(q2[b], cross_w[b, 2 * part : 3 * part, :])
@@ -442,122 +649,107 @@
 
     def leave_cross(i, carry):
         rows = pl.ds(pl.multiple_of(i * quarter, quarter), quarter)
-        grad, gain_cross = norm_back(x1[rows, :], gains_ref[1:2, :], x2[rows, :])
+        grad, gain_cross = norm_back(x1[rows, :], gain_cross_row, x2[rows, :])
         c1[me, rows, :] = (acc[rows, :] + grad).astype(BF16)
         small[0, 1:2, :] += gain_cross
         return carry
 
     lax.fori_loop(0, blocks, leave_cross, 0)
-    arrived(19, rows_recv_x, to_x)
+    arrived(out_x, rows_recv_x, to_x)
     out_ref[...] = (
         rows_low[core, chip].astype(F32)
         + rows_recv[chip].astype(F32)
         + rows_recv_x[...].astype(F32)
     ).astype(BF16)
-    left(15, 19)
-    send(20, c1.at[me], c1.at[me], to_x)
-    send(21, c1.at[me], c1.at[me], to_core)
-
-    def add_rows(ref, start, count, recv, recv_start):
-        at = pl.ds(pl.multiple_of(start, share), count)
-        from_at = pl.ds(pl.multiple_of(recv_start, share), count)
-        ref[at, :] = (ref[at, :].astype(F32) + recv[from_at, :].astype(F32)).astype(BF16)
-
-    def pass_on(ref, base, count, recv, bit, i, recv_next, device):
-        away, kept = (1 - bit) * count, bit * count
-        add_rows(ref, base + away, count, recv, away)
-        rows = pl.ds(pl.multiple_of(base + away, share), count)
-        send(i, ref.at[rows], recv_next, device)
-        add_rows(ref, base + kept, count, recv, kept)
-        return base + kept
-
-    f_base = [None] * 3
-    for i in range(3):
-        arrived(16 + i, f_recv0.at[i], to_y)
-        f_base[i] = pass_on(
-            f_low.at[i], bit_y * half_rows, 2 * share, f_recv0.at[i], bit_z1, 22 + i, f_recv1.at[i], to_z1
-        )
-
-    left(9, 10, 11)
-
-    def memory_grad(target):
-        rows = pl.ds(pl.multiple_of(target * CHUNK, CHUNK), CHUNK)
-        total = None
-        for b in range(blocks):
-            term = dot_nn(kv2[b, rows, :], cross_w[b, lows, :])
-            total = term if total is None else total + term
-        n3[target] = total.astype(BF16)
-
-    memory_grad(by_x)
-    send(25, n3.at[by_x], gm_ref.at[me], to_x)
-    memory_grad(across)
-    send(26, n3.at[across], gm_ref.at[me], to_across)
-    memory_grad(by_core)
-    send(27, n3.at[by_core], gm_ref.at[me], to_core)
-    memory_grad(me)
-    own_rows = pltpu.make_async_copy(n3.at[me], gm_ref.at[me], local_sem.at[9])
-    own_rows.start()
-
-    turn(0, mem[...], 0, "z1")
-    turn(1, n2[...], 0, "z1")
-    turn(1, c2[...], length, "z1")
-    arrived(21, c1.at[by_core], to_core)
+    left(out_core, out_x)
+    c1_x, c1_core, c1_on = fresh(3)
+    send(c1_x, c1.at[me], c1.at[me], to_x)
+    send(c1_core, c1.at[me], c1.at[me], to_core)
+    f_sums[1].step(1)
+    turn(0, mem[...], 0)
+    turn(1, n2[...], 0)
+    turn(1, c2[...], length)
+
+    def put(slabs, first_row, first_col, value):
+        at = 0
+        while at < value.shape[1]:
+            slab, col = divmod(first_col + at, 256)
+            count = min(256 - col, value.shape[1] - at)
+            for i in range(value.shape[0] // share):
+                row = place_of(first_row // share + i, orders[slab]) * share
+                slabs[slab][row : row + share, col : col + count] = value[
+                    i * share : (i + 1) * share, at : at + count
+                ]
+            at += count
 
     def cross_grads(b):
-        for at in range(0, width, half_rows):
-            rows = slice(at, at + half_rows)
-            kv = dot_nn(turned[0, rows, :], kv2[b]).astype(BF16)
-            q = dot_nn(turned[1, rows, 0:length], q2[b]).astype(BF16)
-            o = dot_nn(turned[1, rows, length : 2 * length], o2[b]).astype(BF16)
-            e2[3 * b, rows, :] = kv[:, 0:256]
-            e2[3 * b + 1, rows, 0:128] = kv[:, 256:384]
-            e2[3 * b + 1, rows, 128:256] = q[:, 0:128]
-            e2[3 * b + 2, rows, 0:64] = q[:, 128:192]
-            e2[3 * b + 2, rows, 64:256] = o
-
+        slabs = [e2.at[3 * b + j] for j in range(3)]
+        for at in range(0, width, width // 2):
+            rows = slice(at, at + width // 2)
+            put(slabs, at, 0, dot_nn(turned[0, rows, :], kv2[b]).astype(BF16))
+            put(slabs, at, 2 * part, dot_nn(turned[1, rows, 0:length], q2[b]).astype(BF16))
+            put(slabs, at, 3 * part, dot_nn(turned[1, rows, length : 2 * length], o2[b]).astype(BF16))
+
+    def landing(i, j):
+        return units.at[j, 0:width, 256 * i : 256 * (i + 1)]
+
+    x_core = [fresh(3) for _ in range(2)]
     for i in range(2):
         b = 2 * i + other_core
         cross_grads(b)
+        if i == 0:
+            arrived(c1_core, c1.at[by_core], to_core)
         for j in range(3):
-            send(
-                28 + 3 * i + j,
-                e2.at[3 * b + j, 0:width],
-                units.at[j, 0:width, 256 * i : 256 * (i + 1)],
-                to_core,
-            )
-    arrived(20, c1.at[by_x], to_x)
-    send(34, c1.at[by_x], c1.at[by_x], to_core)
-    for i in range(2):
-        cross_grads(2 * i + core)
+            send(x_core[i][j], e2.at[3 * b + j, 0:width], landing(i, j), to_core)
+    for i in (0, 2):
+        f_sums[i].step(2)
+    x_sums = []
     for i in range(2):
         b = 2 * i + core
-        for j in range(3):
-            arrived(28 + 3 * i + j, units.at[j, 0:width, 256 * i : 256 * (i + 1)], to_core)
-            landed = units.at[j, 0:width, 256 * i : 256 * (i + 1)]
-            mine = e2.at[3 * b + j, 0:width]
-            add_rows(mine, (1 - bit_z1) * half_rows, half_rows, landed, (1 - bit_z1) * half_rows)
-        send(
-            35 + i,
-            e2.at[pl.ds(3 * b, 3), half_at(1 - bit_z1)],
-            x_recv0.at[i],
-            to_z1,
-        )
-        for j in range(3):
-            landed = units.at[j, 0:width, 256 * i : 256 * (i + 1)]
-            mine = e2.at[3 * b + j, 0:width]
-            add_rows(mine, bit_z1 * half_rows, half_rows, landed, bit_z1 * half_rows)
+        cross_grads(b)
+        x_sums.append([
+            Sum(e2.at[3 * b + j], [x_recv0.at[i, j], x_recv1.at[i, j], x_recv2.at[i, j]], orders[j])
+            for j in range(3)
+        ])
+    for j in (0, 2, 1):
+        for i in range(2):
+            arrived(x_core[i][j], landing(i, j), to_core)
+            x_sums[i][j].start_with(landing(i, j))
+
+    left(*n3_x, n3_core, *n3_on)
+    gm_x, gm_across, gm_core = fresh(3)
+
+    def memory_grad(target):
+        rows = pl.ds(pl.multiple_of(target * CHUNK, CHUNK), CHUNK)
+        for at in range(0, width, CHUNK):
+            cols = slice(at, at + CHUNK)
+            total = dot_nn(kv2[0, rows, :], cross_w[0, lows, cols])
+            for b in range(1, blocks):
+                total = total + dot_nn(kv2[b, rows, :], cross_w[b, lows, cols])
+            n3[target, :, cols] = total.astype(BF16)
+
+    memory_grad(by_x)
+    send(gm_x, n3.at[by_x], gm_ref.at[me], to_x)
+    memory_grad(across)
+    send(gm_across, n3.at[across], gm_ref.at[me], to_across)
 
     bias[...] = jnp.zeros_like(bias)
 
     def self_back(t, carry):
-        flip_x, flip_core = lax.div(t, 2), lax.rem(t, 2)
-        at_x = chip + flip_x - 2 * chip * flip_x
-        at_core = core + flip_core - 2 * core * flip_core
-        s = 2 * at_x + at_core
+        s = neighbour(t)
+
+        @pl.when(t == 2)
+        def _():
+            arrived(c1_x, c1.at[by_x], to_x)
+            remote(c1_on, c1.at[by_x], c1.at[by_x], to_core).start()
+            f_sums[1].step(2, True)
 
         @pl.when(t == 3)
         def _():
-            arrived(34, c1.at[across], to_core)
+            arrived(c1_on, c1.at[across], to_core)
+            for i in range(2):
+                x_sums[i][0].step(1, True)
+                x_sums[i][2].step(1, True)
 
         do = dot_nt(wo_ref[...], c1[s])
         dqs = []
@@ -574,7 +766,7 @@
             v1[s, :, cols] = dot_nt(e, low).astype(BF16)
             k1[s, :, cols] = dot_nn(ds, q1[s, :, cols]).astype(BF16)
         q1[s] = jnp.concatenate(dqs, 0).T.astype(BF16)
-        dn = dot_nt(q1[s], wq_ref[...]) + dot_nt(k1[s], wk_ref[...]) + dot_nt(v1[s], wv_ref[...])
+        dn = dot_nn(q1[s], wq_ref[...]) + dot_nn(k1[s], wk_ref[...]) + dot_nn(v1[s], wv_ref[...])
         acc[...] = dn
         for i in range(blocks):
             rows = slice(i * quarter, (i + 1) * quarter)
@@ -584,96 +776,76 @@
         return carry
 
     lax.fori_loop(0, seqs, self_back, 0)
-    send(37, rows_low.at[other_core], rows_recv, to_core)
-    send(38, small.at[0], small_recv.at[0], to_core)
-
-    for s in range(seqs):
-        _, unit = unit_rows(x0_ref[s].astype(F32))
-        turn(0, (unit * gains_ref[0:1, :]).astype(BF16), s * length, "y")
-        turn(1, c1[s], s * length, "y")
-    for keep in (False, True):
-        rows = half_at(bit_y if keep else 1 - bit_y)
-        for i, ref in enumerate((k1, v1, q1, o1)):
-            right = ref[...].reshape(seqs * length, part)
-            value = dot_nn(turned[1 if i == 3 else 0, rows, :], right).astype(BF16)
-            s_low[rows, i * part : (i + 1) * part] = value
-        if not keep:
-            send(39, s_low.at[rows], s_recv0, to_y)
-
-    arrived(37, rows_recv, to_core)
-    rows_send_x[...] = (
-        rows_low[core, other_chip].astype(F32) + rows_recv[other_chip].astype(F32)
-    ).astype(BF16)
-    send(40, rows_send_x, rows_recv_x, to_x)
-    arrived(38, small_recv.at[0], to_core)
-    small[1, 0:8] = small[0] + small_recv[0]
-    send(41, small.at[1], small_recv.at[1], to_x)
+    note(c1_on, c1.at[by_x], c1.at[by_x], to_core, waited=True)
+    note(*f_sums[1].copy(2))
+    for i in range(2):
+        note(*x_sums[i][2].copy(1))
+        note(*x_sums[i][0].copy(1))
+    dn1_core, dn1_x, small_y, small_z1, small_z2 = fresh(5)
+    small_mp = fresh(3)
+    send(dn1_core, rows_low.at[other_core], rows_recv, to_core)
     for h in range(heads):
         total = bias[h]
         step = 1
         while step < length:
             total = jnp.where((key_at & step) != 0, pltpu.roll(total, length - step, 1), total)
             step *= 2
-        small[3, h : h + 1, 0:length] = jnp.sum(total, 0, keepdims=True)
-    arrived(41, small_recv.at[1], to_x)
-    small[2] = small[1] + small_recv[1]
-    send(42, small.at[pl.ds(2, 2)], small_recv.at[pl.ds(2, 2)], to_y)
-
-    x_base = [None] * 2
+        small[1, h : h + 1, 0:length] = jnp.sum(total, 0, keepdims=True)
+    pairs = [pl.ds(2 * i, 2) for i in range(4)]
+    send(small_y, small.at[pairs[0]], small_recv.at[pairs[0]], to_y)
+
+    for s in range(seqs):
+        _, unit = unit_rows(x0_ref[s].astype(F32))
+        turn(0, (unit * gain_self_row).astype(BF16), s * length)
+        turn(1, c1[s], s * length)
+    slabs = [s_low.at[j] for j in range(3)]
+    s_sums = [
+        Sum(s_low.at[j], [s_recv0.at[j], s_recv1.at[j], s_recv2.at[j]], orders[j]) for j in range(3)
+    ]
+    for i, ref in enumerate((k1, v1, q1, o1)):
+        right = ref[...].reshape(seqs * length, part)
+        for at in range(0, width, width // 2):
+            value = dot_nn(turned[i // 3, at : at + width // 2, :], right).astype(BF16)
+            put(slabs, at, i * part, value)
+        if i:
+            s_sums[i - 1].start()
+
+    arrived(dn1_core, rows_recv, to_core)
+    rows_send_x[...] = (
+        rows_low[core, other_chip].astype(F32) + rows_recv[other_chip].astype(F32)
+    ).astype(BF16)
+    send(dn1_x, rows_send_x, rows_recv_x, to_x)
+
+    def pass_small(i, came, device, goes, onward):
+        arrived(came, small_recv.at[pairs[i]], device)
+        small[pairs[i + 1]] = small[pairs[i]] + small_recv[pairs[i]]
+        if goes is not None:
+            send(goes, small.at[pairs[i + 1]], small_recv.at[pairs[i + 1]], onward)
+
+    pass_small(0, small_y, to_y, small_z1, to_z1)
+    memory_grad(by_core)
+    send(gm_core, n3.at[by_core], gm_ref.at[me], to_core)
+    memory_grad(me)
+    own_rows = pltpu.make_async_copy(n3.at[me], gm_ref.at[me], local_sem.at[15])
+    own_rows.start()
+
+    for i in range(2):
+        x_sums[i][0].step(2)
+    pass_small(1, small_z1, to_z1, small_z2, to_z2)
+    for i in range(2):
+        x_sums[i][1].step(1)
+    s_sums[2].step(1)
+    for i in range(2):
+        x_sums[i][2].step(2)
+    s_sums[0].step(1)
+    for i in range(2):
+        x_sums[i][1].step(2)
+    s_sums[2].step(2)
+    s_sums[1].step(1)
     for i in range(3):
-        arrived(22 + i, f_recv1.at[i], to_z1)
-        f_base[i] = pass_on(
-            f_low.at[i], f_base[i], share, f_recv1.at[i], bit_z2, 47 + i, f_recv2.at[i], to_z2
-        )
-    for i in range(2):
-        b = 2 * i + core
-        arrived(35 + i, x_recv0.at[i], to_z1)
-        base = bit_z1 * half_rows
-        away, kept = base + (1 - bit_y) * 2 * share, base + bit_y * 2 * share
-        for j in range(3):
-            add_rows(e2.at[3 * b + j], away, 2 * share, x_recv0.at[i, j], (1 - bit_y) * 2 * share)
-        send(
-            50 + i,
-            e2.at[pl.ds(3 * b, 3), pl.ds(pl.multiple_of(away, share), 2 * share)],
-            x_recv1.at[i],
-            to_y,
-        )
-        for j in range(3):
-            add_rows(e2.at[3 * b + j], kept, 2 * share, x_recv0.at[i, j], bit_y * 2 * share)
-        x_base[i] = kept
-
-    arrived(42, small_recv.at[pl.ds(2, 2)], to_y)
-    small[4:6] = small[2:4] + small_recv[2:4]
-    send(44, small.at[pl.ds(4, 2)], small_recv.at[pl.ds(4, 2)], to_z1)
-    arrived(39, s_recv0, to_y)
-    s_base = pass_on(s_low, bit_y * half_rows, 2 * share, s_recv0, bit_z1, 52, s_recv1, to_z1)
-
-    for i in range(2):
-        b = 2 * i + core
-        arrived(50 + i, x_recv1.at[i], to_y)
-        away, kept = x_base[i] + (1 - bit_z2) * share, x_base[i] + bit_z2 * share
-        for j in range(3):
-            add_rows(e2.at[3 * b + j], away, share, x_recv1.at[i, j], (1 - bit_z2) * share)
-        send(
-            53 + i,
-            e2.at[pl.ds(3 * b, 3), pl.ds(pl.multiple_of(away, share), share)],
-            x_recv2.at[i],
-            to_z2,
-        )
-        for j in range(3):
-            add_rows(e2.at[3 * b + j], kept, share, x_recv1.at[i, j], bit_z2 * share)
-        x_base[i] = kept
-
-    base = x_base[0]
-
-    def cross_sum(at):
-        rows = pl.ds(pl.multiple_of(base, share), share)
-        return [
-            e2[3 * (2 * at + core) + j, rows, :].astype(F32) + x_recv2[at, j].astype(F32)
-            for j in range(3)
-        ]
-
-    arrived(40, rows_recv_x, to_x)
+        gf_ref[i] = f_sums[i].total()
+
+    arrived(dn1_x, rows_recv_x, to_x)
     my_rows = pl.ds(pl.multiple_of(me * quarter, quarter), quarter)
     for s in range(seqs):
         dn = (
@@ -681,34 +853,39 @@
             + rows_recv[chip, s].astype(F32)
             + rows_recv_x[s].astype(F32)
         )
-        grad, _ = norm_back(x0_ref[s, my_rows, :].astype(F32), gains_ref[0:1, :], dn)
+        grad, _ = norm_back(x0_ref[s, my_rows, :].astype(F32), gain_self_row, dn)
         gt_ref[s] = (c1[s, my_rows, :].astype(F32) + grad).astype(BF16)
-
-    arrived(44, small_recv.at[pl.ds(4, 2)], to_z1)
-    small[6:8] = small[4:6] + small_recv[4:6]
-    send(46, small.at[pl.ds(6, 2)], small_recv.at[pl.ds(6, 2)], to_z2)
-    arrived(52, s_recv1, to_z1)
-    s_base = pass_on(s_low, s_base, share, s_recv1, bit_z2, 55, s_recv2, to_z2)
+    s_sums[0].step(2)
+    s_sums[1].step(2)
+
+    last_x = next(names)
     for i in range(2):
-        arrived(53 + i, x_recv2.at[i], to_z2)
-    for j, value in enumerate(cross_sum(other_chip)):
-        x_send3[j] = value.astype(BF16)
-    send(56, x_send3, x_recv3, to_x)
-    for i in range(3):
-        arrived(47 + i, f_recv2.at[i], to_z2)
-        rows = pl.ds(pl.multiple_of(f_base[i], share), share)
-        gf_ref[i] = f_low[i, rows, :].astype(F32) + f_recv2[i].astype(F32)
-    arrived(46, small_recv.at[pl.ds(6, 2)], to_z2)
-    small_ref[...] = small[6:8] + small_recv[6:8]
-    arrived(55, s_recv2, to_z2)
-    rows = pl.ds(pl.multiple_of(s_base, share), share)
-    gs_ref[...] = s_low[rows, :].astype(F32) + s_recv2[...].astype(F32)
-    arrived(56, x_recv3, to_x)
-    for j, value in enumerate(cross_sum(chip)):
-        gx_ref[j] = value + x_recv3[j].astype(F32)
-    arrived(25, gm_ref.at[by_x], to_x)
-    arrived(26, gm_ref.at[across], to_across)
-    arrived(27, gm_ref.at[by_core], to_core)
+        for j in range(3):
+            arrived(x_sums[i][j].ids[2], x_recv2.at[i, j], to_z2)
+
+    def cross_total(at, j):
+        rows = x_sums[0][j].kept[2]
+        return e2[3 * (2 * at + core) + j, rows, :].astype(F32) + x_recv2[at, j].astype(F32)
+
+    for j in range(3):
+        x_send3[j] = cross_total(other_chip, j).astype(BF16)
+    send(last_x, x_send3, x_recv3, to_x)
+    pass_small(2, small_z2, to_z2, None, None)
+    mp_peers = (to_core, to_x, to_across)
+    for i, device in enumerate(mp_peers):
+        send(small_mp[i], small.at[6], small_recv.at[6 + i], device)
+    for j in range(3):
+        gs_ref[j] = s_sums[j].total()
+    arrived(last_x, x_recv3, to_x)
+    for j in range(3):
+        gx_ref[j] = cross_total(chip, j) + x_recv3[j].astype(F32)
+    for i, device in enumerate(mp_peers):
+        arrived(small_mp[i], small_recv.at[6 + i], device)
+    small_ref[0] = small[6] + small_recv[6] + small_recv[7] + small_recv[8]
+    small_ref[1] = small[7]
+    arrived(gm_x, gm_ref.at[by_x], to_x)
+    arrived(gm_across, gm_ref.at[across], to_across)
+    arrived(gm_core, gm_ref.at[by_core], to_core)
     own_rows.wait()
     for copy in sent.values():
         copy.wait_send()
@@ -717,19 +894,23 @@
 def finish_kernel(
     gf_ref, gx_ref, gs_ref, small_ref, onehot_ref, out_ref, gt_ref, gm_ref,
     out_o, gt_o, gm_o, sq_o, sk_o, sv_o, so_o, cq_o, ck_o, cv_o, co_o, gg_o, gu_o, gd_o,
-    gains_o, bias_o,
+    gain_self_o, gain_cross_o, gain_ffn_o, bias_o,
 ):
-    part = sq_o.shape[1]
+    part, share = sq_o.shape[1], sq_o.shape[0]
+    width = small_ref.shape[2]
     out_o[...], gt_o[...], gm_o[...] = out_ref[...], gt_ref[...], gm_ref[...]
-    gg_o[...], gu_o[...], gd_o[...] = gf_ref[0], gf_ref[1], gf_ref[2].T
-    whole = jnp.concatenate([gx_ref[0], gx_ref[1], gx_ref[2]], 1)
-    for value, refs in ((whole, (ck_o, cv_o, cq_o, co_o)), (gs_ref[...], (sk_o, sv_o, sq_o, so_o))):
+    gg_o[...], gu_o[...], gd_o[...] = gf_ref[0], gf_ref[1], gf_ref[2]
+    for source, refs in ((gx_ref, (ck_o, cv_o, cq_o, co_o)), (gs_ref, (sk_o, sv_o, sq_o, so_o))):
+        value = jnp.concatenate([source[0], source[1], source[2]], 1)
         for i in range(3):
             refs[i][...] = value[:, i * part : (i + 1) * part]
         refs[3][...] = value[:, 3 * part :].T
-    gains_o[...] = small_ref[0]
+    shift = width - lax.axis_index("dp") * share
+    gains = pltpu.roll(small_ref[0], shift, 1)
+    for i, ref in enumerate((gain_self_o, gain_cross_o, gain_ffn_o)):
+        ref[...] = gains[i : i + 1, 0:share]
     bias_o[...] = lax.dot_general(
-        onehot_ref[...], small_ref[1, :, 0 : onehot_ref.shape[0]], (((0,), (1,)), ((), ())),
+        small_ref[1, 0 : bias_o.shape[0], 0 : onehot_ref.shape[0]], onehot_ref[...], (((1,), (0,)), ((), ())),
         precision=lax.Precision.HIGHEST, preferred_element_type=F32,
     )
 
@@ -775,9 +956,6 @@
     onehot = jnp.asarray(
         (bucket_table(length)[:, 0][:, None] == np.arange(BUCKETS)[None, :]).astype(np.float32)
     )
-    dist = jnp.dot(onehot, pos_bias, precision=lax.Precision.HIGHEST).T
-    gains = jnp.stack([gain_self, gain_cross, gain_ffn])
-
     def low(*shape):
         return pltpu.VMEM(shape, BF16)
 
@@ -793,7 +971,8 @@
         full(seqs, heads, HEAD_DIM, length), low(seqs, length, part), full(heads, length, length),
         low(3, length, width), low(3, length, width), low(3, length, width),
         full(length, width),
-        low(slots, width), low(seqs, length, width),
+        low(seqs, length, width), low(part, width), low(part, width), low(part, width),
+        low(part, width), low(slots, width), low(seqs, length, width),
         low(width, units), low(width, units), low(units, width), low(blocks, 4 * part, width),
         full(length, width), full(length, width), low(length, width), low(blocks, length, part),
         low(blocks, slots, 2 * part), low(head_all, slots, length), full(head_all, 1, length),
@@ -805,9 +984,9 @@
         low(3, width, units), *sums(3, units),
         low(2, 3, 4 * share, 256), low(2, 3, 2 * share, 256), low(2, 3, share, 256),
         low(3, share, 256), low(3, share, 256),
-        low(width, width), low(4 * share, width), low(2 * share, width), low(share, width),
-        full(8, 8, width), full(8, 8, width),
-        pltpu.SemaphoreType.DMA((19,)),
+        low(3, width, 256), *sums(3, 256),
+        full(8, 8, width), full(9, 8, width),
+        pltpu.SemaphoreType.DMA((16,)),
         pltpu.SemaphoreType.DMA((COPIES,)),
         pltpu.SemaphoreType.DMA((COPIES,)),
     ]
@@ -821,10 +1000,10 @@
             struct((seqs, slots // blocks, width), BF16),
             struct((3, share, units), F32),
             struct((3, share, 256), F32),
-            struct((share, width), F32),
+            struct((3, share, 256), F32),
             struct((2, 8, width), F32),
         ],
-        in_specs=[SMEM] * 2 + [VMEM] * 7 + [ANY] * 9,
+        in_specs=[SMEM] * 3 + [VMEM] * 3 + [ANY] * 14,
         out_specs=[VMEM, VMEM, ANY, VMEM, VMEM, VMEM, VMEM],
         scratch_shapes=scratch,
         compiler_params=pltpu.CompilerParams(
@@ -833,31 +1012,33 @@
         cost_estimate=pl.CostEstimate(flops=24 * 10**9, bytes_accessed=2**24, transcendentals=0),
         name="layer",
     )(
-        target_len, memory_len, targets, query_self, key_self, value_self, out_self, gains, dist,
-        memory, cotangent, query_cross, key_cross, value_cross, out_cross,
+        target_len, memory_len, pos_bias.T,
+        gain_self, gain_cross, gain_ffn, targets,
+        query_self.T, key_self.T, value_self.T, out_self, memory, cotangent, query_cross.T, key_cross.T, value_cross.T, out_cross,
         gate_proj, up_proj, down_proj,
     )
     square = struct((share, part), F32)
     turned = struct((part, share), F32)
     (
-        out, gt, gm, sq, sk, sv, so, cq, ck, cv, co, gg, gu, gd, gains, bias,
+        out, gt, gm, sq, sk, sv, so, cq, ck, cv, co, gg, gu, gd,
+        grad_self, grad_cross, grad_ffn, bias,
     ) = pl.pallas_call(
         finish_kernel,
         out_shape=[
             rows, rows, struct((seqs, slots // blocks, width), BF16),
             square, square, square, turned, square, square, square, turned,
-            struct((share, units), F32), struct((share, units), F32), struct((units, share), F32),
-            struct((8, width), F32), struct((BUCKETS, 8), F32),
+            struct((share, units), F32), struct((share, units), F32), struct((share, units), F32),
+            struct((1, share), F32), struct((1, share), F32), struct((1, share), F32),
+            struct((heads, BUCKETS), F32),
         ],
         in_specs=[VMEM] * 8,
-        out_specs=[VMEM] * 16,
-        compiler_params=pltpu.CompilerParams(vmem_limit_bytes=32 * 2**20),
+        out_specs=[VMEM] * 18,
+        compiler_params=pltpu.CompilerParams(vmem_limit_bytes=62 * 2**20),
         name="finish",
     )(gf, gx, gs, small, onehot, out, gt, gm)
-    gains = lax.dynamic_slice_in_dim(gains[:3], lax.axis_index("dp") * share, share, 1)
     return (
-        out, gt, gm, sq, sk, sv, so, cq, ck, cv, co, gg, gu, gd,
-        gains[0], gains[1], gains[2], bias[:, :heads],
+        out, gt, gm, sq, sk, sv, so, cq, ck, cv, co, gg, gu, gd.T,
+        grad_self[0], grad_cross[0], grad_ffn[0], bias.T,
     )
 
 

time: 194 us -> 142 us (0.73)
  Pallas kernels: 175 us -> 141 us
  local copies, waits for them, and re-layouts: 16.9 us -> 0 us
    pallas_call x1, Pallas kernels: 173 us -> 137 us  [on_device(): pl.pallas_call(layer_kernel, out_shape=[rows, rows, struct((seqs, slots /...]
    unnamed x40 -> x0, local copies, waits for them, and re-layouts: 16.2 us -> none
    pallas_call x1, Pallas kernels: 2.13 us -> 4.14 us  [on_device(): pl.pallas_call(finish_kernel, out_shape=[rows, rows, struct((seqs, slots...]
where the time goes in v1:
time: 142 us
  Pallas kernels  141 us (99%)
    pallas_call x1, Pallas kernels, on_device(): pl.pallas_call(layer_kernel, out_shape=[rows, rows, struct((seqs, slots /...  137 us
    pallas_call x1, Pallas kernels, on_device(): pl.pallas_call(finish_kernel, out_shape=[rows, rows, struct((seqs, slots...  4.14 us

profile of v1, /device:TPU:0, one launch (start us, length us, event | category | flops | bytes accessed | tf_op | source)
XLA Modules:
  0.0 141.6 jit_solution(4432497486769298675)
XLA Ops:
  0.7 136.6 %layer.1 = (bf16[4,64,768]{2,1,0:T(8,128)(2,1)}, bf16[4,64,768]{2,1,0:T(8,128)(2,1)}, bf16[4,256,768]{2,1,0:T(8,128)(2,1)}, f32[3,96,512]{2,1,0:T(8,128)}, f32[3...) custom-call(s32[4]{0:T(128)} %tlen_ref.1, s32[4]{0:T(128)} %mlen_ref.1, f32[3,32]{1,0:T(4,128)} %bitcast.19, ...), custom_call_target="tpu_custom_call" | custom-call | flops 24000000000 | bytes 16777216 | tf_op jit(solution)/shard_map/layer/pallas_call | solution.py:995
  137.3 4.1 %finish.1 = (bf16[4,64,768]{2,1,0:T(8,128)(2,1)}, bf16[4,64,768]{2,1,0:T(8,128)(2,1)}, bf16[4,256,768]{2,1,0:T(8,128)(2,1)}, f32[96,192]{1,0:T(8,128)}, f32[96,1...) custom-call(f32[3,96,512]{2,1,0:T(8,128)} %get-tuple-element.43.gf_r, ...), custom_call_target="tpu_custom_call" | custom-call | tf_op jit(solution)/shard_map/finish/pallas_call | solution.py:1025

commit v2 on v1

--- a/solution.py
+++ b/solution.py
@@ -27,7 +27,8 @@
 F32 = jnp.float32
 BF16 = jnp.bfloat16
 CHUNK = 256
-COPIES = 120
+SPAN = 512
+COPIES = 128
 
 
 def dot(left, right, left_dim, right_dim):
@@ -84,8 +85,8 @@
     x1, x2, n2, q2, kv2, e2, r2, u2, o2,
     n3, units, rows_low, rows_recv, rows_send_x, rows_recv_x,
     c2, turned, c1, f_low, f_recv0, f_recv1, f_recv2,
-    x_recv0, x_recv1, x_recv2, x_send3, x_recv3,
-    s_low, s_recv0, s_recv1, s_recv2, small, small_recv,
+    x_recv0, x_recv1, x_recv2, x_send3, x_recv3, x_mid,
+    s_low, s_recv1, s_recv2, small, small_recv,
     local_sem, send_sem, recv_sem,
 ):
     me = lax.axis_index("mp")
@@ -108,7 +109,6 @@
     blocks = cross_w.shape[0]
     share = width // 8
     quarter = length // blocks
-    half = length // 2
 
     gain_self_row, gain_cross_row, gain_ffn_row = (
         ref[...].reshape(1, width) for ref in (gain_self_ref, gain_cross_ref, gain_ffn_ref)
@@ -225,7 +225,7 @@
     def piece(flip_y, flip_z1, p):
         at_y = bit_y + flip_y * (1 - 2 * bit_y)
         at_z1 = bit_z1 + flip_z1 * (1 - 2 * bit_z1)
-        start = part * (at_y + 2 * at_z1) + share * p
+        start = 2 * part * p + share * (at_y + 2 * at_z1)
         return pl.ds(pl.multiple_of(start, share), share)
 
     lows, highs = slice(0, 2 * part), slice(2 * part, 4 * part)
@@ -262,17 +262,15 @@
             weights_on(w_y[2], from_z1, to_y)
         weights_on(w_on[4 + p], from_z1, to_core)
 
-    def weights_far():
-        weights_from(w_z1[2], piece(1, 1, 0), to_z1)
-        weights_on(w_on[6], piece(1, 1, 0), to_core)
-        weights_from(w_y[2], piece(1, 1, 1), to_y)
-        weights_on(w_on[7], piece(1, 1, 1), to_core)
-
-    def weights_from_core():
+    def weights_far(p):
+        i, device = ((w_z1[2], to_z1), (w_y[2], to_y))[p]
+        weights_from(i, piece(1, 1, p), device)
+        weights_on(w_on[6 + p], piece(1, 1, p), to_core)
+
+    def weights_from_core(p):
         for i, (flip_y, flip_z1) in enumerate(((0, 0), (1, 0), (0, 1), (1, 1))):
-            for p in range(2):
-                rows = piece(flip_y, flip_z1, p)
-                arrived(w_on[2 * i + p], cross_w.at[across, rows], to_core)
+            rows = piece(flip_y, flip_z1, p)
+            arrived(w_on[2 * i + p], cross_w.at[across, rows], to_core)
 
     for p in range(2):
         rows = piece(0, 0, p)
@@ -390,8 +388,10 @@
         return carry
 
     lax.fori_loop(0, blocks, enter_cross, 0)
-    weights_far()
+    weights_far(0)
+    weights_far(1)
     slot_at = lax.broadcasted_iota(jnp.int32, (CHUNK, length), 0)
+    spans = range(0, slots, SPAN)
 
     def cross_one(t, carry):
         b = neighbour(t)
@@ -402,7 +402,8 @@
 
         @pl.when(t == 3)
         def _():
-            weights_from_core()
+            weights_from_core(0)
+            weights_from_core(1)
             keys_values(across)
 
         q = dot_nt(n2[...], cross_w[b, 2 * part : 3 * part, :]).astype(BF16)
@@ -439,18 +440,34 @@
 
     lax.fori_loop(0, blocks, cross_one, 0)
 
-    n3_x, n3_core, n3_on = fresh(2), next(names), fresh(2)
-    dn_near, dn_core, dn_x = next(names), fresh(2), fresh(2)
-    halves = [slice(0, half), slice(half, length)]
+    n3_x, n3_core, n3_on = fresh(blocks), next(names), fresh(blocks)
+    dn_near, dn_core, dn_x = next(names), fresh(blocks), fresh(blocks)
+
+    def quarter_at(i):
+        return pl.ds(pl.multiple_of(i * quarter, quarter), quarter)
+
+    def n3_to_x(i):
+        return (n3_x[0] + i, n3.at[me, quarter_at(i)], n3.at[me, quarter_at(i)], to_x)
+
+    def n3_to_core(i):
+        return (n3_on[0] + i, n3.at[by_x, quarter_at(i)], n3.at[by_x, quarter_at(i)], to_core)
+
+    def dn_to_core(i):
+        rows = quarter_at(i)
+        return (dn_core[0] + i, part_send.at[1, rows], dn_recv.at[1, rows], to_core)
+
+    def dn_to_x(i):
+        return (dn_x[0] + i, part_send.at[2, quarter_at(i)], dn_recv.at[2, quarter_at(i)], to_x)
 
     def enter_ffn(i, carry):
-        rows = pl.ds(pl.multiple_of(i * quarter, quarter), quarter)
+        rows = quarter_at(i)
         n3[me, rows, :] = (unit_rows(x2[rows, :])[1] * gain_ffn_row).astype(BF16)
+        remote(*n3_to_x(i)).start()
         return carry
 
-    for i in range(2):
-        lax.fori_loop(2 * i, 2 * i + 2, enter_ffn, 0)
-        send(n3_x[i], n3.at[me, halves[i]], n3.at[me, halves[i]], to_x)
+    lax.fori_loop(0, blocks, enter_ffn, 0)
+    for i in range(blocks):
+        note(*n3_to_x(i), waited=True)
     send(n3_core, n3.at[me], n3.at[me], to_core)
     for load in loads[10:]:
         load.wait()
@@ -470,50 +487,8 @@
     def turn_normed(s):
         turn(0, n3[s], pl.multiple_of(s * length, length), "y")
 
-    def pass_dn(i):
-        arrived(dn_core[i], dn_recv.at[1, halves[i]], to_core)
-        part_send[2, halves[i], :] = (
-            part_send[2, halves[i], :].astype(F32) + dn_recv[1, halves[i], :].astype(F32)
-        ).astype(BF16)
-        remote(dn_x[i], part_send.at[2, halves[i]], dn_recv.at[2, halves[i]], to_x).start()
-
-    def ffn_one(t, carry):
-        late, odd = lax.div(t, 2), lax.rem(t, 2)
-        at_x = chip + late * (other_chip - chip)
-        near_core = (1 - late) * odd
-        seq_a = 2 * at_x + core + near_core * (other_core - core)
-        seq_b = 2 * at_x + core + (late + near_core) * (other_core - core)
-        half_a, half_b = late * odd, 1 - late + late * odd
-        in_a = pl.ds(pl.multiple_of(half_a * half, half), half)
-        in_b = pl.ds(pl.multiple_of(half_b * half, half), half)
-        rows_a = pl.ds(pl.multiple_of(seq_a * length + half_a * half, half), half)
-        rows_b = pl.ds(pl.multiple_of(seq_b * length + half_b * half, half), half)
-
-        @pl.when(t == 1)
-        def _():
-            arrived(n3_core, n3.at[by_core], to_core)
-
-        @pl.when(t == 2)
-        def _():
-            turn_normed(me)
-            turn_normed(by_core)
-            arrived(n3_x[0], n3.at[by_x, halves[0]], to_x)
-            remote(n3_on[0], n3.at[by_x, halves[0]], n3.at[by_x, halves[0]], to_core).start()
-            turn(1, cot[0], 0, "z1")
-            turn(1, cot[1], length, "z1")
-            arrived(n3_on[0], n3.at[across, halves[0]], to_core)
-
-        @pl.when(t == 3)
-        def _():
-            pass_dn(0)
-            arrived(n3_x[1], n3.at[by_x, halves[1]], to_x)
-            remote(n3_on[1], n3.at[by_x, halves[1]], n3.at[by_x, halves[1]], to_core).start()
-            turn(1, cot[2], 2 * length, "z1")
-            turn(1, cot[3], 3 * length, "z1")
-            arrived(n3_on[1], n3.at[across, halves[1]], to_core)
-
-        n = jnp.concatenate([n3[seq_a, in_a, :], n3[seq_b, in_b, :]], 0)
-        c = jnp.concatenate([cot[seq_a, in_a, :], cot[seq_b, in_b, :]], 0)
+    def ffn_rows(n, c, at_rows):
+        count = n.shape[0] // len(at_rows)
         for at in range(0, wg.shape[1], CHUNK):
             cols = slice(at, at + CHUNK)
             a = dot_nn(n, wg[:, cols])
@@ -526,13 +501,24 @@
             rise = mid + 0.5 * a * (1.0 - slope * slope) * (scale * (1.0 + 3.0 * cubic * square))
             for i, value in enumerate((dh * b * rise, dh * gelu, gelu * b)):
                 value = value.astype(BF16)
-                units[i, rows_a, cols] = value[:half]
-                units[i, rows_b, cols] = value[half:]
-
-        def both(i):
-            return jnp.concatenate([units[i, rows_a, :], units[i, rows_b, :]], 0)
-
-        dn = dot_nt(both(0), wg[...]) + dot_nt(both(1), wu[...])
+                for j, rows in enumerate(at_rows):
+                    units[i, rows, cols] = value[j * count : (j + 1) * count]
+
+        def whole(i):
+            return jnp.concatenate([units[i, rows, :] for rows in at_rows], 0)
+
+        dn = dot_nt(whole(0), wg[...]) + dot_nt(whole(1), wu[...])
+        return dn, lambda: dot_nn(whole(2), wd[...])
+
+    def ffn_near(t, carry):
+        s = neighbour(t)
+
+        @pl.when(t == 1)
+        def _():
+            arrived(n3_core, n3.at[by_core], to_core)
+
+        rows = pl.ds(pl.multiple_of(s * length, length), length)
+        dn, result = ffn_rows(n3[s], cot[s], [rows])
 
         @pl.when(t == 0)
         def _():
@@ -543,33 +529,58 @@
             part_send[0] = dn.astype(BF16)
             remote(dn_near, part_send.at[0], dn_recv.at[0], to_core).start()
 
-        for i in range(2):
-
-            @pl.when(t == 2 + i)
-            def _(i=i):
-                part_send[1, halves[i], :] = dn[half:].astype(BF16)
-                remote(
-                    dn_core[i], part_send.at[1, halves[i]], dn_recv.at[1, halves[i]], to_core
-                ).start()
-                part_send[2, halves[i], :] = dn[:half].astype(BF16)
-
         own = jnp.where(t == 0, 1.0, 0.0)
-        result = (dot_nn(both(2), wd[...]) + own * x2[...]).astype(BF16)
-        rows_low[0, half_a, seq_a] = result[0:quarter]
-        rows_low[1, half_a, seq_a] = result[quarter : 2 * quarter]
-        rows_low[0, half_b, seq_b] = result[2 * quarter : 3 * quarter]
-        rows_low[1, half_b, seq_b] = result[3 * quarter :]
+        low = (result() + own * x2[...]).astype(BF16)
+        for i in range(blocks):
+            rows_low[i % 2, i // 2, s] = low[i * quarter : (i + 1) * quarter]
         return carry
 
-    lax.fori_loop(0, seqs, ffn_one, 0)
-    pass_dn(1)
-    for i in range(2):
-        note(n3_on[i], n3.at[by_x, halves[i]], n3.at[by_x, halves[i]], to_core, waited=True)
-        note(
-            dn_core[i], part_send.at[1, halves[i]], dn_recv.at[1, halves[i]], to_core, waited=True
+    lax.fori_loop(0, 2, ffn_near, 0)
+    note(dn_near, part_send.at[0], dn_recv.at[0], to_core)
+    turn_normed(me)
+    turn_normed(by_core)
+
+    def pass_dn(i):
+        rows = quarter_at(i)
+        arrived(dn_core[0] + i, dn_recv.at[1, rows], to_core)
+        part_send[2, rows, :] = (
+            part_send[2, rows, :].astype(F32) + dn_recv[1, rows, :].astype(F32)
+        ).astype(BF16)
+        remote(*dn_to_x(i)).start()
+
+    def ffn_far(t, carry):
+        rows = quarter_at(t)
+
+        @pl.when(t > 0)
+        def _():
+            pass_dn(t - 1)
+
+        arrived(n3_x[0] + t, n3.at[by_x, rows], to_x)
+        remote(*n3_to_core(t)).start()
+        turn(1, cot[t], pl.multiple_of(t * length, length), "z1")
+        arrived(n3_on[0] + t, n3.at[across, rows], to_core)
+        n = jnp.concatenate([n3[by_x, rows, :], n3[across, rows, :]], 0)
+        c = jnp.concatenate([cot[by_x, rows, :], cot[across, rows, :]], 0)
+        dn, result = ffn_rows(
+            n, c, [
+                pl.ds(pl.multiple_of(s * length + t * quarter, quarter), quarter)
+                for s in (by_x, across)
+            ],
         )
-        note(dn_x[i], part_send.at[2, halves[i]], dn_recv.at[2, halves[i]], to_x)
-    note(dn_near, part_send.at[0], dn_recv.at[0], to_core)
+        part_send[1, rows, :] = dn[quarter:].astype(BF16)
+        remote(*dn_to_core(t)).start()
+        part_send[2, rows, :] = dn[:quarter].astype(BF16)
+        low = result().astype(BF16)
+        rows_low[lax.rem(t, 2), lax.div(t, 2), by_x] = low[:quarter]
+        rows_low[lax.rem(t, 2), lax.div(t, 2), across] = low[quarter:]
+        return carry
+
+    lax.fori_loop(0, blocks, ffn_far, 0)
+    pass_dn(blocks - 1)
+    for i in range(blocks):
+        note(*n3_to_core(i), waited=True)
+        note(*dn_to_core(i), waited=True)
+        note(*dn_to_x(i))
     out_core, out_x = fresh(2)
     send(out_core, rows_low.at[other_core], rows_recv, to_core)
     turn_normed(by_x)
@@ -595,8 +606,8 @@
     send(out_x, rows_send_x, rows_recv_x, to_x)
 
     arrived(dn_near, dn_recv.at[0], to_core)
-    for i in range(2):
-        arrived(dn_x[i], dn_recv.at[2, halves[i]], to_x)
+    for i in range(blocks):
+        arrived(dn_x[i], dn_recv.at[2, quarter_at(i)], to_x)
     small[...] = jnp.zeros_like(small)
 
     def enter_back(i, carry):
@@ -612,9 +623,12 @@
     lax.fori_loop(0, blocks, enter_back, 0)
 
     def cross_back(b, carry):
+        @pl.when(b == 2)
+        def _():
+            f_sums[0].step(1, True)
+
         @pl.when(b == 3)
         def _():
-            f_sums[0].step(1, True)
             f_sums[2].step(1, True)
 
         do = dot_nt(cross_w[b, 3 * part : 4 * part, :], c2[...])
@@ -627,11 +641,11 @@
             low = (do[cols] * r).astype(BF16)
             delta = r * jnp.sum(low.astype(F32) * u2[b * heads + h], 0, keepdims=True)
             dq = jnp.zeros((HEAD_DIM, length), F32)
-            for at in range(0, slots, CHUNK):
-                rows = slice(at, at + CHUNK)
+            for at in spans:
+                rows = slice(at, at + SPAN)
                 e = e2[b * heads + h, rows, :]
                 dp = dot_nn(kv2[b, rows, cols_v], low)
-                ds = (e.astype(F32) * (dp - delta)).astype(BF16)
+                ds = e * (dp - delta).astype(BF16)
                 dq = dq + dot_tn(kv2[b, rows, cols], ds)
                 kv2[b, rows, cols_v] = dot_nt(e, low).astype(BF16)
                 kv2[b, rows, cols] = dot_nn(ds, q[:, cols]).astype(BF16)
@@ -694,27 +708,51 @@
         return units.at[j, 0:width, 256 * i : 256 * (i + 1)]
 
     x_core = [fresh(3) for _ in range(2)]
-    for i in range(2):
+    x_sums = [
+        [
+            Sum(
+                e2.at[3 * (2 * i + core) + j],
+                [x_recv0.at[i, j], x_recv1.at[i, j], x_recv2.at[i, j]],
+                orders[j],
+            )
+            for j in range(3)
+        ]
+        for i in range(2)
+    ]
+    mid_sum = Sum(
+        e2.at[3 * (2 * chip + core) + 1], [x_mid, x_recv1.at[0, 1], x_recv2.at[0, 1]], "y"
+    )
+    mid_x = fresh(2)
+    mid_halves = [slice(0, 4 * share), slice(4 * share, 8 * share)]
+
+    def cross_away(i):
         b = 2 * i + other_core
         cross_grads(b)
         if i == 0:
             arrived(c1_core, c1.at[by_core], to_core)
         for j in range(3):
             send(x_core[i][j], e2.at[3 * b + j, 0:width], landing(i, j), to_core)
+
+    def cross_start(i):
+        for j in (0, 2):
+            arrived(x_core[i][j], landing(i, j), to_core)
+            x_sums[i][j].start_with(landing(i, j))
+        arrived(x_core[i][1], landing(i, 1), to_core)
+        for rows in mid_halves:
+            add_rows(e2.at[3 * (2 * i + core) + 1], rows, landing(i, 1), rows)
+
+    cross_away(0)
+    cross_grads(core)
+    cross_away(1)
+    cross_start(0)
     for i in (0, 2):
         f_sums[i].step(2)
-    x_sums = []
+    cross_grads(2 + core)
+    cross_start(1)
     for i in range(2):
-        b = 2 * i + core
-        cross_grads(b)
-        x_sums.append([
-            Sum(e2.at[3 * b + j], [x_recv0.at[i, j], x_recv1.at[i, j], x_recv2.at[i, j]], orders[j])
-            for j in range(3)
-        ])
-    for j in (0, 2, 1):
-        for i in range(2):
-            arrived(x_core[i][j], landing(i, j), to_core)
-            x_sums[i][j].start_with(landing(i, j))
+        send(
+            mid_x[i], e2.at[3 * (2 * other_chip + core) + 1, mid_halves[i]], x_recv0.at[i, 1], to_x
+        )
 
     left(*n3_x, n3_core, *n3_on)
     gm_x, gm_across, gm_core = fresh(3)
@@ -743,13 +781,14 @@
             arrived(c1_x, c1.at[by_x], to_x)
             remote(c1_on, c1.at[by_x], c1.at[by_x], to_core).start()
             f_sums[1].step(2, True)
+            x_sums[0][0].step(1, True)
+            x_sums[0][2].step(1, True)
 
         @pl.when(t == 3)
         def _():
             arrived(c1_on, c1.at[across], to_core)
-            for i in range(2):
-                x_sums[i][0].step(1, True)
-                x_sums[i][2].step(1, True)
+            x_sums[1][0].step(1, True)
+            x_sums[1][2].step(1, True)
 
         do = dot_nt(wo_ref[...], c1[s])
         dqs = []
@@ -760,7 +799,7 @@
             delta = r * jnp.sum(low.astype(F32) * u1[s, h], 0, keepdims=True)
             e = e1[s, h]
             dp = dot_nn(v1[s, :, cols], low)
-            ds = (e.astype(F32) * (dp - delta)).astype(BF16)
+            ds = e * (dp - delta).astype(BF16)
             bias[h] += ds.astype(F32)
             dqs.append(dot_tn(k1[s, :, cols], ds))
             v1[s, :, cols] = dot_nt(e, low).astype(BF16)
@@ -784,15 +823,18 @@
     dn1_core, dn1_x, small_y, small_z1, small_z2 = fresh(5)
     small_mp = fresh(3)
     send(dn1_core, rows_low.at[other_core], rows_recv, to_core)
+    for i in range(2):
+        arrived(mid_x[i], x_recv0.at[i, 1], to_x)
+        add_rows(e2.at[3 * (2 * chip + core) + 1], mid_halves[i], x_recv0.at[i, 1], slice(None))
+    mid_sum.start()
     for h in range(heads):
         total = bias[h]
         step = 1
         while step < length:
             total = jnp.where((key_at & step) != 0, pltpu.roll(total, length - step, 1), total)
             step *= 2
-        small[1, h : h + 1, 0:length] = jnp.sum(total, 0, keepdims=True)
-    pairs = [pl.ds(2 * i, 2) for i in range(4)]
-    send(small_y, small.at[pairs[0]], small_recv.at[pairs[0]], to_y)
+        small[0, 3 + h : 4 + h, 0:length] = jnp.sum(total, 0, keepdims=True)
+    send(small_y, small.at[0], small_recv.at[0], to_y)
 
     for s in range(seqs):
         _, unit = unit_rows(x0_ref[s].astype(F32))
@@ -800,7 +842,7 @@
         turn(1, c1[s], s * length)
     slabs = [s_low.at[j] for j in range(3)]
     s_sums = [
-        Sum(s_low.at[j], [s_recv0.at[j], s_recv1.at[j], s_recv2.at[j]], orders[j]) for j in range(3)
+        Sum(s_low.at[j], [f_recv0.at[j, :, 0:256], s_recv1.at[j], s_recv2.at[j]], orders[j]) for j in range(3)
     ]
     for i, ref in enumerate((k1, v1, q1, o1)):
         right = ref[...].reshape(seqs * length, part)
@@ -809,6 +851,9 @@
             put(slabs, at, i * part, value)
         if i:
             s_sums[i - 1].start()
+        if i == 2:
+            x_sums[0][0].step(2)
+            x_sums[1][0].step(2)
 
     arrived(dn1_core, rows_recv, to_core)
     rows_send_x[...] = (
@@ -817,34 +862,49 @@
     send(dn1_x, rows_send_x, rows_recv_x, to_x)
 
     def pass_small(i, came, device, goes, onward):
-        arrived(came, small_recv.at[pairs[i]], device)
-        small[pairs[i + 1]] = small[pairs[i]] + small_recv[pairs[i]]
+        arrived(came, small_recv.at[i], device)
+        small[i + 1] = small[i] + small_recv[i]
         if goes is not None:
-            send(goes, small.at[pairs[i + 1]], small_recv.at[pairs[i + 1]], onward)
-
-    pass_small(0, small_y, to_y, small_z1, to_z1)
+            send(goes, small.at[i + 1], small_recv.at[i + 1], onward)
+
+    mid_sum.step(1)
     memory_grad(by_core)
     send(gm_core, n3.at[by_core], gm_ref.at[me], to_core)
     memory_grad(me)
     own_rows = pltpu.make_async_copy(n3.at[me], gm_ref.at[me], local_sem.at[15])
     own_rows.start()
-
-    for i in range(2):
-        x_sums[i][0].step(2)
-    pass_small(1, small_z1, to_z1, small_z2, to_z2)
-    for i in range(2):
-        x_sums[i][1].step(1)
+    pass_small(0, small_y, to_y, small_z1, to_z1)
+
     s_sums[2].step(1)
     for i in range(2):
         x_sums[i][2].step(2)
+    mid_sum.step(2)
     s_sums[0].step(1)
-    for i in range(2):
-        x_sums[i][1].step(2)
+    pass_small(1, small_z1, to_z1, small_z2, to_z2)
+    s_sums[1].step(1)
     s_sums[2].step(2)
-    s_sums[1].step(1)
+    s_sums[0].step(2)
     for i in range(3):
         gf_ref[i] = f_sums[i].total()
 
+    s_sums[1].step(2)
+
+    last_x = next(names)
+    for i in range(2):
+        for j in (0, 2):
+            arrived(x_sums[i][j].ids[2], x_recv2.at[i, j], to_z2)
+
+    def cross_total(at, j):
+        rows = x_sums[0][j].kept[2]
+        return e2[3 * (2 * at + core) + j, rows, :].astype(F32) + x_recv2[at, j].astype(F32)
+
+    for i, j in enumerate((0, 2)):
+        x_send3[i] = cross_total(other_chip, j).astype(BF16)
+    send(last_x, x_send3, x_recv3, to_x)
+    pass_small(2, small_z2, to_z2, None, None)
+    mp_peers = (to_core, to_x, to_across)
+    for i, device in enumerate(mp_peers):
+        send(small_mp[i], small.at[3], small_recv.at[3 + i], device)
     arrived(dn1_x, rows_recv_x, to_x)
     my_rows = pl.ds(pl.multiple_of(me * quarter, quarter), quarter)
     for s in range(seqs):
@@ -855,34 +915,16 @@
         )
         grad, _ = norm_back(x0_ref[s, my_rows, :].astype(F32), gain_self_row, dn)
         gt_ref[s] = (c1[s, my_rows, :].astype(F32) + grad).astype(BF16)
-    s_sums[0].step(2)
-    s_sums[1].step(2)
-
-    last_x = next(names)
-    for i in range(2):
-        for j in range(3):
-            arrived(x_sums[i][j].ids[2], x_recv2.at[i, j], to_z2)
-
-    def cross_total(at, j):
-        rows = x_sums[0][j].kept[2]
-        return e2[3 * (2 * at + core) + j, rows, :].astype(F32) + x_recv2[at, j].astype(F32)
-
-    for j in range(3):
-        x_send3[j] = cross_total(other_chip, j).astype(BF16)
-    send(last_x, x_send3, x_recv3, to_x)
-    pass_small(2, small_z2, to_z2, None, None)
-    mp_peers = (to_core, to_x, to_across)
-    for i, device in enumerate(mp_peers):
-        send(small_mp[i], small.at[6], small_recv.at[6 + i], device)
     for j in range(3):
         gs_ref[j] = s_sums[j].total()
     arrived(last_x, x_recv3, to_x)
-    for j in range(3):
-        gx_ref[j] = cross_total(chip, j) + x_recv3[j].astype(F32)
+    for i, j in enumerate((0, 2)):
+        gx_ref[j] = cross_total(chip, j) + x_recv3[i].astype(F32)
+    gx_ref[1] = mid_sum.total()
     for i, device in enumerate(mp_peers):
-        arrived(small_mp[i], small_recv.at[6 + i], device)
-    small_ref[0] = small[6] + small_recv[6] + small_recv[7] + small_recv[8]
-    small_ref[1] = small[7]
+        arrived(small_mp[i], small_recv.at[3 + i], device)
+    small_ref[0] = small[3] + small_recv[3] + small_recv[4] + small_recv[5]
+    small_ref[1] = small[3]
     arrived(gm_x, gm_ref.at[by_x], to_x)
     arrived(gm_across, gm_ref.at[across], to_across)
     arrived(gm_core, gm_ref.at[by_core], to_core)
@@ -910,7 +952,7 @@
     for i, ref in enumerate((gain_self_o, gain_cross_o, gain_ffn_o)):
         ref[...] = gains[i : i + 1, 0:share]
     bias_o[...] = lax.dot_general(
-        small_ref[1, 0 : bias_o.shape[0], 0 : onehot_ref.shape[0]], onehot_ref[...], (((1,), (0,)), ((), ())),
+        small_ref[1, 3 : 3 + bias_o.shape[0], 0 : onehot_ref.shape[0]], onehot_ref[...], (((1,), (0,)), ((), ())),
         precision=lax.Precision.HIGHEST, preferred_element_type=F32,
     )
 
@@ -983,9 +1025,9 @@
         low(length, width), low(2, width, seqs * length), low(seqs, length, width),
         low(3, width, units), *sums(3, units),
         low(2, 3, 4 * share, 256), low(2, 3, 2 * share, 256), low(2, 3, share, 256),
-        low(3, share, 256), low(3, share, 256),
-        low(3, width, 256), *sums(3, 256),
-        full(8, 8, width), full(9, 8, width),
+        low(2, share, 256), low(2, share, 256), low(4 * share, 256),
+        low(3, width, 256), *sums(3, 256)[1:],
+        full(4, 8, width), full(6, 8, width),
         pltpu.SemaphoreType.DMA((16,)),
         pltpu.SemaphoreType.DMA((COPIES,)),
         pltpu.SemaphoreType.DMA((COPIES,)),

time: 142 us -> 138 us (0.972)
  Pallas kernels: 141 us -> 137 us
    pallas_call x1, Pallas kernels: 137 us -> 133 us  [on_device(): pl.pallas_call(layer_kernel, out_shape=[rows, rows, struct((seqs, slots /...]
where the time goes in v2:
time: 138 us
  Pallas kernels  137 us (99%)
    pallas_call x1, Pallas kernels, on_device(): pl.pallas_call(layer_kernel, out_shape=[rows, rows, struct((seqs, slots /...  133 us
    pallas_call x1, Pallas kernels, on_device(): pl.pallas_call(finish_kernel, out_shape=[rows, rows, struct((seqs, slots...  4.14 us

profile of v2, /device:TPU:0, one launch (start us, length us, event | category | flops | bytes accessed | tf_op | source)
XLA Modules:
  0.0 137.9 jit_solution(10610659460588155774)
XLA Ops:
  0.7 132.9 %layer.1 = (bf16[4,64,768]{2,1,0:T(8,128)(2,1)}, bf16[4,64,768]{2,1,0:T(8,128)(2,1)}, bf16[4,256,768]{2,1,0:T(8,128)(2,1)}, f32[3,96,512]{2,1,0:T(8,128)}, f32[3...) custom-call(s32[4]{0:T(128)} %tlen_ref.1, s32[4]{0:T(128)} %mlen_ref.1, f32[3,32]{1,0:T(4,128)} %bitcast.19, ...), custom_call_target="tpu_custom_call" | custom-call | flops 24000000000 | bytes 16777216 | tf_op jit(solution)/shard_map/layer/pallas_call | solution.py:1037
  133.6 4.1 %finish.1 = (bf16[4,64,768]{2,1,0:T(8,128)(2,1)}, bf16[4,64,768]{2,1,0:T(8,128)(2,1)}, bf16[4,256,768]{2,1,0:T(8,128)(2,1)}, f32[96,192]{1,0:T(8,128)}, f32[96,1...) custom-call(f32[3,96,512]{2,1,0:T(8,128)} %get-tuple-element.43.gf_r, ...), custom_call_target="tpu_custom_call" | custom-call | tf_op jit(solution)/shard_map/finish/pallas_call | solution.py:1067

commit v3 on v2

--- a/solution.py
+++ b/solution.py
@@ -823,10 +823,6 @@
     dn1_core, dn1_x, small_y, small_z1, small_z2 = fresh(5)
     small_mp = fresh(3)
     send(dn1_core, rows_low.at[other_core], rows_recv, to_core)
-    for i in range(2):
-        arrived(mid_x[i], x_recv0.at[i, 1], to_x)
-        add_rows(e2.at[3 * (2 * chip + core) + 1], mid_halves[i], x_recv0.at[i, 1], slice(None))
-    mid_sum.start()
     for h in range(heads):
         total = bias[h]
         step = 1
@@ -835,6 +831,10 @@
             step *= 2
         small[0, 3 + h : 4 + h, 0:length] = jnp.sum(total, 0, keepdims=True)
     send(small_y, small.at[0], small_recv.at[0], to_y)
+    for i in range(2):
+        arrived(mid_x[i], x_recv0.at[i, 1], to_x)
+        add_rows(e2.at[3 * (2 * chip + core) + 1], mid_halves[i], x_recv0.at[i, 1], slice(None))
+    mid_sum.start()
 
     for s in range(seqs):
         _, unit = unit_rows(x0_ref[s].astype(F32))
@@ -844,16 +844,17 @@
     s_sums = [
         Sum(s_low.at[j], [f_recv0.at[j, :, 0:256], s_recv1.at[j], s_recv2.at[j]], orders[j]) for j in range(3)
     ]
-    for i, ref in enumerate((k1, v1, q1, o1)):
+    for i, ref in ((2, q1), (3, o1), (0, k1), (1, v1)):
         right = ref[...].reshape(seqs * length, part)
         for at in range(0, width, width // 2):
             value = dot_nn(turned[i // 3, at : at + width // 2, :], right).astype(BF16)
             put(slabs, at, i * part, value)
-        if i:
-            s_sums[i - 1].start()
-        if i == 2:
+        if i == 3:
+            s_sums[2].start()
             x_sums[0][0].step(2)
             x_sums[1][0].step(2)
+    s_sums[0].start()
+    s_sums[1].start()
 
     arrived(dn1_core, rows_recv, to_core)
     rows_send_x[...] = (

time: 138 us -> 137 us (level)
  no operation moved by 1% of the time
where the time goes in v3:
time: 137 us
  Pallas kernels  136 us (99%)
    pallas_call x1, Pallas kernels, on_device(): pl.pallas_call(layer_kernel, out_shape=[rows, rows, struct((seqs, slots /...  132 us
    pallas_call x1, Pallas kernels, on_device(): pl.pallas_call(finish_kernel, out_shape=[rows, rows, struct((seqs, slots...  4.14 us

profile of v3, /device:TPU:0, one launch (start us, length us, event | category | flops | bytes accessed | tf_op | source)
XLA Modules:
  0.0 137.2 jit_solution(8282643288168646513)
XLA Ops:
  0.7 132.2 %layer.1 = (bf16[4,64,768]{2,1,0:T(8,128)(2,1)}, bf16[4,64,768]{2,1,0:T(8,128)(2,1)}, bf16[4,256,768]{2,1,0:T(8,128)(2,1)}, f32[3,96,512]{2,1,0:T(8,128)}, f32[3...) custom-call(s32[4]{0:T(128)} %tlen_ref.1, s32[4]{0:T(128)} %mlen_ref.1, f32[3,32]{1,0:T(4,128)} %bitcast.19, ...), custom_call_target="tpu_custom_call" | custom-call | flops 24000000000 | bytes 16777216 | tf_op jit(solution)/shard_map/layer/pallas_call | solution.py:1038
  132.9 4.1 %finish.1 = (bf16[4,64,768]{2,1,0:T(8,128)(2,1)}, bf16[4,64,768]{2,1,0:T(8,128)(2,1)}, bf16[4,256,768]{2,1,0:T(8,128)(2,1)}, f32[96,192]{1,0:T(8,128)}, f32[96,1...) custom-call(f32[3,96,512]{2,1,0:T(8,128)} %get-tuple-element.43.gf_r, ...), custom_call_target="tpu_custom_call" | custom-call | tf_op jit(solution)/shard_map/finish/pallas_call | solution.py:1068
